TPU v7x, 128 devices: a whole 4x4x4 slice. The times are simulated.
128 devices in a mesh: seq: 8 (over x, z_lo), dp: 16 (over z_hi, y, core).
Axes of the slice: x: 4, y: 4, z: 4 (z_hi: 2, z_lo: 2; z = z_hi * 2 + z_lo), core: 2. Of those that a mesh axis runs over, the one named last changes fastest.
Arguments:
- query_in: bfloat16 [16, 32, 64, 1536], P('dp', 'seq'), may hold values from -8 to 8
- key_in: bfloat16 [16, 32, 64, 1536], P('dp', 'seq'), may hold values from -8 to 8
- value_in: bfloat16 [16, 32, 64, 1536], P('dp', 'seq'), may hold values from -5 to 5
- cotangent: bfloat16 [16, 32, 64, 3072], P('dp', 'seq'), may hold values from -5 to 5
- out_weight: bfloat16 [1536, 3072], P(('seq', 'dp')), may hold values from -0.15625 to 0.15625
Outputs:
- grad_query: bfloat16 [16, 32, 64, 1536], P('dp', 'seq')
- grad_key: bfloat16 [16, 32, 64, 1536], P('dp', 'seq')
- grad_value: bfloat16 [16, 32, 64, 1536], P('dp', 'seq')
- grad_weight: float32 [1536, 3072], P(('seq', 'dp'))
All inputs are finite; a program needn't handle non-finite values.
Results may differ from a plain program's by a relative error of at most 0.0073.
Values may be sent and summed in bfloat16 or wider, within the bound.
A program may use at most 128 MiB of HBM per device.

v0:
```python
import math

import jax
import jax.numpy as jnp
from jax import lax
from jax.sharding import PartitionSpec as P

HEADS = 12
HDIM = 128


def attend(query_s, key_s, value_s, score_scale):
    score = (
        jnp.einsum("cfshe,cgshe->cshfg", query_s, key_s, preferred_element_type=jnp.float32)
        * score_scale
    )
    attn_prob = jax.nn.softmax(score, axis=-1)
    prob_low = attn_prob.astype(jnp.bfloat16)
    attn_out = jnp.einsum(
        "cshfg,cgshe->cfshe", prob_low, value_s, preferred_element_type=jnp.float32
    )
    return (attn_prob, prob_low, attn_out.astype(jnp.bfloat16))


def attend_back(query_s, key_s, value_s, attn_prob, prob_low, d_head, score_scale):
    grad_value = jnp.einsum(
        "cshfg,cfshe->cgshe", prob_low, d_head, preferred_element_type=jnp.float32
    )
    d_prob = jnp.einsum("cfshe,cgshe->cshfg", d_head, value_s, preferred_element_type=jnp.float32)
    d_score = attn_prob * (d_prob - jnp.sum(attn_prob * d_prob, axis=-1, keepdims=True))
    score_low = d_score.astype(jnp.bfloat16)
    grad_query = (
        jnp.einsum("cshfg,cgshe->cfshe", score_low, key_s, preferred_element_type=jnp.float32)
        * score_scale
    )
    grad_key = (
        jnp.einsum("cshfg,cfshe->cgshe", score_low, query_s, preferred_element_type=jnp.float32)
        * score_scale
    )
    return (
        grad_query.astype(jnp.bfloat16),
        grad_key.astype(jnp.bfloat16),
        grad_value.astype(jnp.bfloat16),
    )


def local(query_in, key_in, value_in, cotangent, out_weight):
    score_scale = 1.0 / math.sqrt(HDIM)
    clip_count, frame_dev, space_all, feature_all = query_in.shape
    model_width = cotangent.shape[3]
    head_shape = (clip_count, frame_dev, space_all, HEADS, HDIM)
    token_dev = clip_count * frame_dev * space_all
    tokens_total = token_dev * lax.axis_size("seq") * lax.axis_size("dp")
    query_s, key_s, value_s = (
        lax.all_to_all(
            query_in.reshape(head_shape), "seq", split_axis=2, concat_axis=1, tiled=True
        ),
        lax.all_to_all(key_in.reshape(head_shape), "seq", split_axis=2, concat_axis=1, tiled=True),
        lax.all_to_all(
            value_in.reshape(head_shape), "seq", split_axis=2, concat_axis=1, tiled=True
        ),
    )
    attn_prob, prob_low, attn_out = attend(query_s, key_s, value_s, score_scale)
    out_time = lax.all_to_all(attn_out, "seq", split_axis=1, concat_axis=2, tiled=True)
    out_flat = out_time.reshape(token_dev, feature_all)
    cot_flat = cotangent.reshape(token_dev, model_width)
    d_out = jnp.einsum(
        "td,rd->tr",
        cot_flat,
        lax.all_gather(out_weight, ("seq", "dp"), axis=0, tiled=True),
        preferred_element_type=jnp.float32,
    ).astype(jnp.bfloat16)
    d_head = lax.all_to_all(
        d_out.reshape(head_shape), "seq", split_axis=2, concat_axis=1, tiled=True
    )
    weight_term = jnp.einsum("tr,td->rd", out_flat, cot_flat, preferred_element_type=jnp.float32)
    weight_sum = lax.psum_scatter(weight_term, ("seq", "dp"), scatter_dimension=0, tiled=True)
    grad_weight = weight_sum * (1.0 / math.sqrt(tokens_total))
    grad_query, grad_key, grad_value = attend_back(
        query_s, key_s, value_s, attn_prob, prob_low, d_head, score_scale
    )
    back_query, back_key, back_value = (
        lax.all_to_all(grad_query, "seq", split_axis=1, concat_axis=2, tiled=True),
        lax.all_to_all(grad_key, "seq", split_axis=1, concat_axis=2, tiled=True),
        lax.all_to_all(grad_value, "seq", split_axis=1, concat_axis=2, tiled=True),
    )
    flat_shape = (clip_count, frame_dev, space_all, feature_all)
    return (
        back_query.reshape(flat_shape),
        back_key.reshape(flat_shape),
        back_value.reshape(flat_shape),
        grad_weight,
    )


def solution(mesh):
    in_specs = (
        P("dp", "seq", None, None),
        P("dp", "seq", None, None),
        P("dp", "seq", None, None),
        P("dp", "seq", None, None),
        P(("seq", "dp"), None),
    )
    out_specs = (
        P("dp", "seq", None, None),
        P("dp", "seq", None, None),
        P("dp", "seq", None, None),
        P(("seq", "dp"), None),
    )
    return jax.shard_map(local, mesh=mesh, in_specs=in_specs, out_specs=out_specs, check_vma=False)
```

profile of v0, /device:TPU:3, one launch (start us, length us, event | category | flops | bytes accessed | tf_op | source)
XLA Modules:
  0.0 912.2 jit_solution(4529038751260869857)
XLA Ops:
  11.5 5.6 all-to-all-start
  20.6 8.9 all-to-all-done
  29.5 5.1 all-to-all-start.1
  38.1 9.5 %all-to-all-done.1 = bf16[1,4,64,12,128]{4,1,3,0,2:T(4,128)(2,1)} async-done(((bf16[1,4,64,12,128]{4,1,3,0,2:T(4,128)(2,1)}), bf16[1,4,64,12,128]{4,1,3,0,2:T(4,128)(2,1)}, u32[]{:S(2)}, u32[]{:S(2)}) %all-to-all-start.1) | async-done | bytes 786464 | tf_op jit(solution)/shard_map/all_to_all | solution.py:58
  47.5 5.5 all-to-all-start.3
  56.7 9.0 all-to-all-done.3
  71.9 19.0 %all_to_all.120 = bf16[1,32,8,12,128]{4,2,3,0,1:T(8,128)(2,1)S(1)} all-to-all(bf16[1,32,8,12,128]{4,2,3,0,1:T(8,128)(2,1)S(1)} %copy.89), channel_id=1, replica_groups=mesh['seq'=8,'dp'=16] {'seq'}, dimensions={1} | all-to-all | bytes 1572864 | tf_op jit(solution)/shard_map/all_to_all | solution.py:64
  91.0 8.0 fusion.13
  99.0 135.9 %all-gather.3.cloned.1.call-done = bf16[128,12,3072]{2,1,0:T(8,128)(2,1)} async-done(((bf16[1,12,3072]{2,1,0:T(8,128)(2,1)}), bf16[128,12,3072]{2,1,0:T(8,128)(2,1)}) %all-gather.3.cloned.1.call-update) | async-done | bytes 9437200 | tf_op jit(solution)/shard_map/all_gather | solution.py:70
  234.9 13.7 %reshape.123 = bf16[1536,3072]{1,0:T(8,128)(2,1)} reshape(bf16[128,12,3072]{2,1,0:T(8,128)(2,1)} %all-gather.3.cloned.1.call-done) | data formatting | bytes 18874368
  248.6 7.2 convolution_convert_fusion
  259.3 4.4 all-to-all-start.2
  263.7 323.5 %fusion = f32[16,3072]{1,0:T(8,128)S(1)} fusion(f32[1536,3072]{1,0:T(8,128)} %fusion.13), kind=kCustom, calls=%all-reduce-scatter | all-reduce-scatter fusion | flops 6291457 | bytes 19070976
  587.2 9.1 collective-permute-start.30
  598.2 24.5 %collective-permute-start.28 = (f32[16,3072]{1,0:T(8,128)S(1)}, f32[16,3072]{1,0:T(8,128)}, u32[]{:S(2)}, u32[]{:S(2)}) collective-permute-start(f32[16,3072]{1,0:T(8,128)S(1)} %fusion), channel_id=1, source_target_pairs={{0,29},{1,30},{2,31},{3,32},{4,33},{5,34},{6,35},{7,36},{8,37},{9,... | collective-permute-start | bytes 589832
  624.6 10.8 %collective-permute-start.31 = (f32[12,3072]{1,0:T(8,128)S(1)}, f32[12,3072]{1,0:T(8,128)}, u32[]{:S(2)}, u32[]{:S(2)}) collective-permute-start(f32[12,3072]{1,0:T(8,128)S(1)} %slice), channel_id=1, source_target_pairs={{0,32},{1,33},{2,34},{3,35},{4,36},{5,37},{6,38},{7,39},{8,40},{9,... | collective-permute-start | bytes 442376
  639.7 6.3 all-to-all-start.6
  650.3 14.2 %collective-permute-start.25 = (f32[16,3072]{1,0:T(8,128)S(1)}, f32[16,3072]{1,0:T(8,128)S(1)}, u32[]{:S(2)}, u32[]{:S(2)}) collective-permute-start(f32[16,3072]{1,0:T(8,128)S(1)} %fusion), channel_id=1, source_target_pairs={{0,26},{1,27},{2,28},{3,29},{4,30},{5,31},{6,32},{7,33},{8,34},{9,... | collective-permute-start | bytes 589832
  678.0 9.1 all-to-all-start.5
  687.1 4.4 collective-permute-start.19
  691.5 3.9 collective-permute-start.18
  695.5 4.6 collective-permute-start.17
  704.6 11.5 %collective-permute-done.19 = f32[16,3072]{1,0:T(8,128)S(1)} collective-permute-done((f32[16,3072]{1,0:T(8,128)S(1)}, f32[16,3072]{1,0:T(8,128)S(1)}, u32[]{:S(2)}, u32[]{:S(2)}) %collective-permute-start.19) | collective-permute-done | bytes 196640
  717.9 7.3 collective-permute-done.18
  725.3 6.2 collective-permute-start.13
  731.5 10.3 %collective-permute-start.12 = (f32[16,3072]{1,0:T(8,128)S(1)}, f32[16,3072]{1,0:T(8,128)S(1)}, u32[]{:S(2)}, u32[]{:S(2)}) collective-permute-start(f32[16,3072]{1,0:T(8,128)S(1)} %fusion), channel_id=1, source_target_pairs={{0,13},{1,14},{2,15},{3,16},{4,17},{5,18},{6,19},{7,20},{8,21},{9,... | collective-permute-start | bytes 589832
  743.8 10.6 %collective-permute-start.10 = (f32[16,3072]{1,0:T(8,128)S(1)}, f32[16,3072]{1,0:T(8,128)S(1)}, u32[]{:S(2)}, u32[]{:S(2)}) collective-permute-start(f32[16,3072]{1,0:T(8,128)S(1)} %fusion), channel_id=1, source_target_pairs={{0,11},{1,12},{2,13},{3,14},{4,15},{5,16},{6,17},{7,18},{8,19},{9,... | collective-permute-start | bytes 589832
  758.2 6.8 collective-permute-start.8
  765.1 9.4 %collective-permute-start.7 = (f32[16,3072]{1,0:T(8,128)S(1)}, f32[16,3072]{1,0:T(8,128)}, u32[]{:S(2)}, u32[]{:S(2)}) collective-permute-start(f32[16,3072]{1,0:T(8,128)S(1)} %fusion), channel_id=1, source_target_pairs={{0,8},{1,9},{2,10},{3,11},{4,12},{5,13},{6,14},{7,15},{8,16},{9,17... | collective-permute-start | bytes 589832
  788.8 6.1 collective-permute-start.3
  807.1 7.0 collective-permute-done.2
  815.5 85.3 %concatenate = f32[524,3072]{1,0:T(8,128)} concatenate(f32[12,3072]{1,0:T(8,128)} %collective-permute-done.31, f32[16,3072]{1,0:T(8,128)} %collective-permute-done.30, f32[16,3072]{1,0:T(8,128)} %collective-permute-done.29, f32[16,3072]{1,0:T(8,128)} %collective-permute-done.28, f32[16,3072]{1,0:T(8,128)} %collective-permute-done.27, f32[16,3072]{1,0:T(8,128)S(1)} %collective-permute-done.26, ...), dimensions={0} | concatenate | bytes 12877824
  (135 shorter events, 94.7 us)
Async XLA Ops:
  7.2 227.7 %all-gather.3.cloned.1.call-start = ((), (), s32[]{:S(2)}) async-start(), calls=%async_computation.8 | async-start | bytes 12681216 | tf_op jit(solution)/shard_map/all_gather | solution.py:70
  259.3 376.1 %all-to-all-start.2 = ((bf16[1,4,64,12,128]{4,1,3,0,2:T(4,128)(2,1)}), bf16[1,4,64,12,128]{4,1,3,0,2:T(4,128)(2,1)S(1)}, u32[]{:S(2)}, u32[]{:S(2)}) async-start(bf16[1,4,64,12,128]{4,1,3,0,2:T(4,128)(2,1)} %copy.76), calls=%async_computation.2 | async-start | bytes 1572864 | tf_op jit(solution)/shard_map/all_to_all | solution.py:73
  587.2 63.1 %collective-permute-start.30 = (f32[16,3072]{1,0:T(8,128)S(1)}, f32[16,3072]{1,0:T(8,128)}, u32[]{:S(2)}, u32[]{:S(2)}) collective-permute-start(f32[16,3072]{1,0:T(8,128)S(1)} %fusion), channel_id=1, source_target_pairs={{0,31},{1,32},{2,33},{3,34},{4,35},{5,36},{6,37},{7,38},{8,39},{9,... | collective-permute-start | bytes 589832
  596.3 68.8 %collective-permute-start.29 = (f32[16,3072]{1,0:T(8,128)S(1)}, f32[16,3072]{1,0:T(8,128)}, u32[]{:S(2)}, u32[]{:S(2)}) collective-permute-start(f32[16,3072]{1,0:T(8,128)S(1)} %fusion), channel_id=1, source_target_pairs={{0,30},{1,31},{2,32},{3,33},{4,34},{5,35},{6,36},{7,37},{8,38},{9,... | collective-permute-start | bytes 589832
  598.2 68.8 %collective-permute-start.28 = (f32[16,3072]{1,0:T(8,128)S(1)}, f32[16,3072]{1,0:T(8,128)}, u32[]{:S(2)}, u32[]{:S(2)}) collective-permute-start(f32[16,3072]{1,0:T(8,128)S(1)} %fusion), channel_id=1, source_target_pairs={{0,29},{1,30},{2,31},{3,32},{4,33},{5,34},{6,35},{7,36},{8,37},{9,... | collective-permute-start | bytes 589832
  622.7 46.2 %collective-permute-start.27 = (f32[16,3072]{1,0:T(8,128)S(1)}, f32[16,3072]{1,0:T(8,128)}, u32[]{:S(2)}, u32[]{:S(2)}) collective-permute-start(f32[16,3072]{1,0:T(8,128)S(1)} %fusion), channel_id=1, source_target_pairs={{0,28},{1,29},{2,30},{3,31},{4,32},{5,33},{6,34},{7,35},{8,36},{9,... | collective-permute-start | bytes 589832
  624.6 23.7 %collective-permute-start.31 = (f32[12,3072]{1,0:T(8,128)S(1)}, f32[12,3072]{1,0:T(8,128)}, u32[]{:S(2)}, u32[]{:S(2)}) collective-permute-start(f32[12,3072]{1,0:T(8,128)S(1)} %slice), channel_id=1, source_target_pairs={{0,32},{1,33},{2,34},{3,35},{4,36},{5,37},{6,38},{7,39},{8,40},{9,... | collective-permute-start | bytes 442376
  639.7 38.3 %all-to-all-start.6 = ((bf16[1,32,8,12,128]{4,2,3,0,1:T(8,128)(2,1)}), bf16[1,32,8,12,128]{4,2,3,0,1:T(8,128)(2,1)S(1)}, u32[]{:S(2)}, u32[]{:S(2)}) async-start(bf16[1,32,8,12,128]{4,2,3,0,1:T(8,128)(2,1)} %copy.86), calls=%async_computation.6 | async-start | bytes 1572864 | tf_op jit(solution)/shard_map/all_to_all | solution.py:85
  648.3 22.5 %collective-permute-start.26 = (f32[16,3072]{1,0:T(8,128)S(1)}, f32[16,3072]{1,0:T(8,128)S(1)}, u32[]{:S(2)}, u32[]{:S(2)}) collective-permute-start(f32[16,3072]{1,0:T(8,128)S(1)} %fusion), channel_id=1, source_target_pairs={{0,27},{1,28},{2,29},{3,30},{4,31},{5,32},{6,33},{7,34},{8,35},{9,... | collective-permute-start | bytes 589832
  650.3 22.9 %collective-permute-start.25 = (f32[16,3072]{1,0:T(8,128)S(1)}, f32[16,3072]{1,0:T(8,128)S(1)}, u32[]{:S(2)}, u32[]{:S(2)}) collective-permute-start(f32[16,3072]{1,0:T(8,128)S(1)} %fusion), channel_id=1, source_target_pairs={{0,26},{1,27},{2,28},{3,29},{4,30},{5,31},{6,32},{7,33},{8,34},{9,... | collective-permute-start | bytes 589832
  665.0 22.1 %collective-permute-start.24 = (f32[16,3072]{1,0:T(8,128)S(1)}, f32[16,3072]{1,0:T(8,128)}, u32[]{:S(2)}, u32[]{:S(2)}) collective-permute-start(f32[16,3072]{1,0:T(8,128)S(1)} %fusion), channel_id=1, source_target_pairs={{0,25},{1,26},{2,27},{3,28},{4,29},{5,30},{6,31},{7,32},{8,33},{9,... | collective-permute-start | bytes 589832
  667.0 24.5 %collective-permute-start.23 = (f32[16,3072]{1,0:T(8,128)S(1)}, f32[16,3072]{1,0:T(8,128)}, u32[]{:S(2)}, u32[]{:S(2)}) collective-permute-start(f32[16,3072]{1,0:T(8,128)S(1)} %fusion), channel_id=1, source_target_pairs={{0,24},{1,25},{2,26},{3,27},{4,28},{5,29},{6,30},{7,31},{8,32},{9,... | collective-permute-start | bytes 589832
  668.9 26.5 %collective-permute-start.22 = (f32[16,3072]{1,0:T(8,128)S(1)}, f32[16,3072]{1,0:T(8,128)}, u32[]{:S(2)}, u32[]{:S(2)}) collective-permute-start(f32[16,3072]{1,0:T(8,128)S(1)} %fusion), channel_id=1, source_target_pairs={{0,23},{1,24},{2,25},{3,26},{4,27},{5,28},{6,29},{7,30},{8,31},{9,... | collective-permute-start | bytes 589832
  670.9 29.2 %collective-permute-start.21 = (f32[16,3072]{1,0:T(8,128)S(1)}, f32[16,3072]{1,0:T(8,128)}, u32[]{:S(2)}, u32[]{:S(2)}) collective-permute-start(f32[16,3072]{1,0:T(8,128)S(1)} %fusion), channel_id=1, source_target_pairs={{0,22},{1,23},{2,24},{3,25},{4,26},{5,27},{6,28},{7,29},{8,30},{9,... | collective-permute-start | bytes 589832
  673.2 28.8 %collective-permute-start.20 = (f32[16,3072]{1,0:T(8,128)S(1)}, f32[16,3072]{1,0:T(8,128)}, u32[]{:S(2)}, u32[]{:S(2)}) collective-permute-start(f32[16,3072]{1,0:T(8,128)S(1)} %fusion), channel_id=1, source_target_pairs={{0,21},{1,22},{2,23},{3,24},{4,25},{5,26},{6,27},{7,28},{8,29},{9,... | collective-permute-start | bytes 589832
  678.0 104.4 %all-to-all-start.5 = ((bf16[1,32,8,12,128]{4,2,3,0,1:T(8,128)(2,1)}), bf16[1,32,8,12,128]{4,2,3,0,1:T(8,128)(2,1)S(1)}, u32[]{:S(2)}, u32[]{:S(2)}) async-start(bf16[1,32,8,12,128]{4,2,3,0,1:T(8,128)(2,1)} %copy.84), calls=%async_computation.5 | async-start | bytes 1572864 | tf_op jit(solution)/shard_map/all_to_all | solution.py:84
  687.1 28.9 %collective-permute-start.19 = (f32[16,3072]{1,0:T(8,128)S(1)}, f32[16,3072]{1,0:T(8,128)S(1)}, u32[]{:S(2)}, u32[]{:S(2)}) collective-permute-start(f32[16,3072]{1,0:T(8,128)S(1)} %fusion), channel_id=1, source_target_pairs={{0,20},{1,21},{2,22},{3,23},{4,24},{5,25},{6,26},{7,27},{8,28},{9,... | collective-permute-start | bytes 589832
  691.5 33.7 %collective-permute-start.18 = (f32[16,3072]{1,0:T(8,128)S(1)}, f32[16,3072]{1,0:T(8,128)S(1)}, u32[]{:S(2)}, u32[]{:S(2)}) collective-permute-start(f32[16,3072]{1,0:T(8,128)S(1)} %fusion), channel_id=1, source_target_pairs={{0,19},{1,20},{2,21},{3,22},{4,23},{5,24},{6,25},{7,26},{8,27},{9,... | collective-permute-start | bytes 589832
  695.5 36.1 %collective-permute-start.17 = (f32[16,3072]{1,0:T(8,128)S(1)}, f32[16,3072]{1,0:T(8,128)S(1)}, u32[]{:S(2)}, u32[]{:S(2)}) collective-permute-start(f32[16,3072]{1,0:T(8,128)S(1)} %fusion), channel_id=1, source_target_pairs={{0,18},{1,19},{2,20},{3,21},{4,22},{5,23},{6,24},{7,25},{8,26},{9,... | collective-permute-start | bytes 589832
  700.0 41.8 %collective-permute-start.16 = (f32[16,3072]{1,0:T(8,128)S(1)}, f32[16,3072]{1,0:T(8,128)S(1)}, u32[]{:S(2)}, u32[]{:S(2)}) collective-permute-start(f32[16,3072]{1,0:T(8,128)S(1)} %fusion), channel_id=1, source_target_pairs={{0,17},{1,18},{2,19},{3,20},{4,21},{5,22},{6,23},{7,24},{8,25},{9,... | collective-permute-start | bytes 589832
  702.0 41.8 %collective-permute-start.15 = (f32[16,3072]{1,0:T(8,128)S(1)}, f32[16,3072]{1,0:T(8,128)S(1)}, u32[]{:S(2)}, u32[]{:S(2)}) collective-permute-start(f32[16,3072]{1,0:T(8,128)S(1)} %fusion), channel_id=1, source_target_pairs={{0,16},{1,17},{2,18},{3,19},{4,20},{5,21},{6,22},{7,23},{8,24},{9,... | collective-permute-start | bytes 589832
  716.0 38.4 %collective-permute-start.14 = (f32[16,3072]{1,0:T(8,128)S(1)}, f32[16,3072]{1,0:T(8,128)S(1)}, u32[]{:S(2)}, u32[]{:S(2)}) collective-permute-start(f32[16,3072]{1,0:T(8,128)S(1)} %fusion), channel_id=1, source_target_pairs={{0,15},{1,16},{2,17},{3,18},{4,19},{5,20},{6,21},{7,22},{8,23},{9,... | collective-permute-start | bytes 589832
  725.3 33.0 %collective-permute-start.13 = (f32[16,3072]{1,0:T(8,128)S(1)}, f32[16,3072]{1,0:T(8,128)S(1)}, u32[]{:S(2)}, u32[]{:S(2)}) collective-permute-start(f32[16,3072]{1,0:T(8,128)S(1)} %fusion), channel_id=1, source_target_pairs={{0,14},{1,15},{2,16},{3,17},{4,18},{5,19},{6,20},{7,21},{8,22},{9,... | collective-permute-start | bytes 589832
  731.5 33.5 %collective-permute-start.12 = (f32[16,3072]{1,0:T(8,128)S(1)}, f32[16,3072]{1,0:T(8,128)S(1)}, u32[]{:S(2)}, u32[]{:S(2)}) collective-permute-start(f32[16,3072]{1,0:T(8,128)S(1)} %fusion), channel_id=1, source_target_pairs={{0,13},{1,14},{2,15},{3,16},{4,17},{5,18},{6,19},{7,20},{8,21},{9,... | collective-permute-start | bytes 589832
  741.9 32.6 %collective-permute-start.11 = (f32[16,3072]{1,0:T(8,128)S(1)}, f32[16,3072]{1,0:T(8,128)S(1)}, u32[]{:S(2)}, u32[]{:S(2)}) collective-permute-start(f32[16,3072]{1,0:T(8,128)S(1)} %fusion), channel_id=1, source_target_pairs={{0,12},{1,13},{2,14},{3,15},{4,16},{5,17},{6,18},{7,19},{8,20},{9,... | collective-permute-start | bytes 589832
  743.8 32.6 %collective-permute-start.10 = (f32[16,3072]{1,0:T(8,128)S(1)}, f32[16,3072]{1,0:T(8,128)S(1)}, u32[]{:S(2)}, u32[]{:S(2)}) collective-permute-start(f32[16,3072]{1,0:T(8,128)S(1)} %fusion), channel_id=1, source_target_pairs={{0,11},{1,12},{2,13},{3,14},{4,15},{5,16},{6,17},{7,18},{8,19},{9,... | collective-permute-start | bytes 589832
  754.5 31.5 %collective-permute-start.9 = (f32[16,3072]{1,0:T(8,128)S(1)}, f32[16,3072]{1,0:T(8,128)}, u32[]{:S(2)}, u32[]{:S(2)}) collective-permute-start(f32[16,3072]{1,0:T(8,128)S(1)} %fusion), channel_id=1, source_target_pairs={{0,10},{1,11},{2,12},{3,13},{4,14},{5,15},{6,16},{7,17},{8,18},{9,... | collective-permute-start | bytes 589832
  758.2 30.5 %collective-permute-start.8 = (f32[16,3072]{1,0:T(8,128)S(1)}, f32[16,3072]{1,0:T(8,128)}, u32[]{:S(2)}, u32[]{:S(2)}) collective-permute-start(f32[16,3072]{1,0:T(8,128)S(1)} %fusion), channel_id=1, source_target_pairs={{0,9},{1,10},{2,11},{3,12},{4,13},{5,14},{6,15},{7,16},{8,17},{9,1... | collective-permute-start | bytes 589832
  765.1 29.8 %collective-permute-start.7 = (f32[16,3072]{1,0:T(8,128)S(1)}, f32[16,3072]{1,0:T(8,128)}, u32[]{:S(2)}, u32[]{:S(2)}) collective-permute-start(f32[16,3072]{1,0:T(8,128)S(1)} %fusion), channel_id=1, source_target_pairs={{0,8},{1,9},{2,10},{3,11},{4,12},{5,13},{6,14},{7,15},{8,16},{9,17... | collective-permute-start | bytes 589832
  774.5 24.1 %collective-permute-start.6 = (f32[16,3072]{1,0:T(8,128)S(1)}, f32[16,3072]{1,0:T(8,128)}, u32[]{:S(2)}, u32[]{:S(2)}) collective-permute-start(f32[16,3072]{1,0:T(8,128)S(1)} %fusion), channel_id=1, source_target_pairs={{0,7},{1,8},{2,9},{3,10},{4,11},{5,12},{6,13},{7,14},{8,15},{9,16}... | collective-permute-start | bytes 589832
  777.2 23.3 %collective-permute-start.5 = (f32[16,3072]{1,0:T(8,128)S(1)}, f32[16,3072]{1,0:T(8,128)}, u32[]{:S(2)}, u32[]{:S(2)}) collective-permute-start(f32[16,3072]{1,0:T(8,128)S(1)} %fusion), channel_id=1, source_target_pairs={{0,6},{1,7},{2,8},{3,9},{4,10},{5,11},{6,12},{7,13},{8,14},{9,15},... | collective-permute-start | bytes 589832
  782.4 122.0 %all-to-all-start.4 = ((bf16[1,32,8,12,128]{4,2,3,0,1:T(8,128)(2,1)}), bf16[1,32,8,12,128]{4,2,3,0,1:T(8,128)(2,1)S(1)}, u32[]{:S(2)}, u32[]{:S(2)}) async-start(bf16[1,32,8,12,128]{4,2,3,0,1:T(8,128)(2,1)} %copy.82), calls=%async_computation.4 | async-start | bytes 1572864 | tf_op jit(solution)/shard_map/all_to_all | solution.py:83
  (32 other events, 701.1 us)
Sparse Core Ops, SparseCore 0:
  9.7 225.0 all-gather.2
where the time goes:
time: 920 us; the launch traced here: 912 us
  blocking collectives  342 us (37%)
  starting transfers between devices  205 us (22%)
  waiting for transfers between devices  196 us (21%)
  local copies, waits for them, and re-layouts  128 us (14%)
  matrix products  23.4 us (3%)
  between operations  14.9 us (2%)
    unnamed x1, blocking collectives  323 us
    unnamed x32, starting transfers between devices  166 us
    all_gather x1, waiting for transfers between devices, local(): lax.all_gather(out_weight, ('seq', 'dp'), axis=0, tiled=True)  136 us
    unnamed x51, local copies, waits for them, and re-layouts  101 us
    unnamed x33, waiting for transfers between devices  32.3 us
    all_to_all x1, blocking collectives, local(): lax.all_to_all(attn_out, 'seq', split_axis=1, concat_axis=2, tiled=True)  19 us
  transfers between devices with their start and end apart: 40, of which 10 were waited for; matrix products, arithmetic and copies ran while one was open for 49% of the time, Pallas kernels for 0%

commit v1 on v0

v1 whole, which is shorter than its diff:
```python
import math

import jax
import jax.numpy as jnp
from jax import lax
from jax.experimental import pallas as pl
from jax.experimental.pallas import tpu as pltpu
from jax.sharding import PartitionSpec as P

MESH = pl.DeviceIdType.MESH
F32, BF16 = jnp.float32, jnp.bfloat16

FRAMES, POS, HD, D, HDIM = 32, 16, 1536, 3072, 128
HALF = HD // 2
TOK = FRAMES * POS
HEADS = HALF // HDIM
PK = 2304
COL = 768
ROWS = 512
NAT = 384
NT = (((1,), (1,)), ((), ()))
TN = (((0,), (0,)), ((), ()))


def dot(a, b, dims=(((1,), (0,)), ((), ()))):
    return lax.dot_general(a, b, dims, preferred_element_type=F32)


def kernel(
    q_in, k_in, v_in, c_in, w_in,
    gq_out, gk_out, gv_out, gw_out,
    qb, kb, vb, cb, wp, wn, prob, ao, aot, em, um, part, ry, s1, rz, s2, rf, dob, gqb, gkb, gvb,
    a_ss, a_rs, f_ss, f_rs, w1_ss, w1_rs, w2_ss, w2_rs, w3_ss, w3_rs,
    y_ss, y_rs, z_ss, z_rs, x_ss, x_rs, g_ss, g_rs,
):
    seq, dp = lax.axis_index("seq"), lax.axis_index("dp")
    x, zl = seq // 2, seq % 2
    zh, y, c = dp // 8, (dp // 2) % 4, dp % 2
    z = zh * 2 + zl

    def dev(x, y, z, c):
        return {"seq": x * 2 + z % 2, "dp": (z // 2) * 8 + y * 2 + c}

    def remote(src, dst, ss, rs, to):
        return pltpu.make_async_remote_copy(
            src_ref=src, dst_ref=dst, send_sem=ss, recv_sem=rs, device_id=to, device_id_type=MESH
        )

    def done(ref, sem):
        pltpu.make_async_copy(ref, ref, sem).wait()

    def post(src, dst, ss, rs, to, own=None):
        if own is None:
            remote(src, dst, ss, rs, to).start()
            return

        @pl.when(own)
        def _():
            pltpu.make_async_copy(src, dst, rs).start()

        @pl.when(jnp.logical_not(own))
        def _():
            remote(src, dst, ss, rs, to).start()

    def sent(src, ss, own=None):
        if own is None:
            done(src, ss)
        else:
            pl.when(jnp.logical_not(own))(lambda: done(src, ss))

    barrier = pltpu.get_barrier_semaphore()
    peers = [
        dev((x + dx) % 4, y, zh * 2 + (zl + kz) % 2, (c + kc) % 2)
        for dx in range(4) for kz in range(2) for kc in range(2) if dx or kz or kc
    ]
    peers += [dev(x, y, (z + 2) % 4, c), dev(x, y, ((z + 2) % 4) // 2 * 2 + (zl + 1) % 2, c)]
    peers += [dev(x, (y + dy) % 4, z, c) for dy in range(1, 4)]
    for to in peers:
        pl.semaphore_signal(barrier, inc=1, device_id=to, device_id_type=MESH)
    pl.semaphore_wait(barrier, len(peers))

    half = x // 2
    w_own = c == half
    w_slot = wp.at[x % 2, y, z, pl.ds(pl.multiple_of(c * 16, 16), 16), :]

    def w1_args(dx):
        return (w_in, w_slot, w1_ss.at[dx], w1_rs.at[(x % 2) * 2 + c], dev((x + dx) % 4, y, z, half))

    for dx in range(4):
        post(*w1_args(dx), own=w_own if dx == 0 else None)

    a_own = zl == c
    mine = pl.ds(pl.multiple_of(seq * 4, 4), 4)

    def a_args(arr, dx, kc):
        px, core = (x + dx) % 4, (c + kc) % 2
        to = dev(px, y, zh * 2 + c, core)
        pos = pl.ds(pl.multiple_of(px * 16, 16), 16)
        if arr < 3:
            col = pl.ds(pl.multiple_of(core * HALF, HALF), HALF)
            src = (q_in, k_in, v_in)[arr].at[:, pos, col]
            dst = (qb, kb, vb)[arr].at[mine]
        else:
            col = pl.ds(pl.multiple_of(core * HD, HD), HD)
            src = c_in.at[:, pos, col]
            dst = cb.at[mine, :, col]
        return src, dst, a_ss.at[arr, dx * 2 + kc], a_rs.at[arr, seq], to

    def a_each(fn):
        for arr in range(4):
            for dx in (2, 1, 3, 0):
                for kc in range(2):
                    fn(arr, dx, kc, a_own if dx == 0 and kc == 0 else None)

    a_each(lambda arr, dx, kc, own: post(*a_args(arr, dx, kc), own=own))

    def packed(shape, axis):
        m = lax.broadcasted_iota(jnp.int32, shape, axis)
        j, r = m >> 4, m & 15
        owner = ((j >> 1) & 1) * 16 + ((j >> 2) & 1) * 8 + (j >> 3) * 2 + (j & 1)
        return owner * 12, r

    base, r = packed((ROWS, NAT), 0)
    n = lax.broadcasted_iota(jnp.int32, (ROWS, NAT), 1)
    for p in range(3):
        hit = n == jnp.where(r < 12, base + r, base + (r - 12 + 4 * p))
        em[p] = jnp.where(hit, 1.0, 0.0).astype(BF16)
    base, r = packed((NAT, ROWS), 1)
    n = lax.broadcasted_iota(jnp.int32, (NAT, ROWS), 0)
    um[0] = jnp.where(n == jnp.where(r < 12, base + r, -1), 1.0, 0.0).astype(BF16)
    for p in range(3):
        hit = n == jnp.where(r < 12, -1, base + (r - 12 + 4 * p))
        um[p + 1] = jnp.where(hit, 1.0, 0.0).astype(BF16)

    for i in range(4):
        done(wp.at[i // 2, y, z, pl.ds((i % 2) * 16, 16), :], w1_rs.at[i])

    def w2_args(dz):
        blk = wp.at[:, y, z]
        return (blk, blk, w2_ss.at[dz - 1], w2_rs.at[z], dev(x, y, (z + dz) % 4, c))

    for dz in range(1, 4):
        post(*w2_args(dz))

    def w3_args(dz, dy):
        zz = (z + dz) % 4
        blk = wp.at[:, y, zz]
        return (blk, blk, w3_ss.at[dz * 3 + dy - 1], w3_rs.at[y * 4 + zz], dev(x, (y + dy) % 4, z, c))

    for dz in (0, 1, 3, 2):
        if dz:
            zz = (z + dz) % 4
            done(wp.at[:, y, zz], w2_rs.at[zz])
        for dy in (2, 1, 3):
            post(*w3_args(dz, dy))

    for s in range(8):
        for arr, buf in enumerate((qb, kb, vb)):
            done(buf.at[pl.ds(s * 4, 4)], a_rs.at[arr, s])

    scale = 1.0 / math.sqrt(HDIM)

    def head(buf, h):
        return buf[:, :, pl.ds(pl.multiple_of(h * HDIM, HDIM), HDIM)].reshape(TOK, HDIM)

    def forward(h, _):
        score = dot(head(qb, h), head(kb, h), NT) * scale
        row = lax.broadcasted_iota(jnp.int32, (TOK, TOK), 0)
        col = lax.broadcasted_iota(jnp.int32, (TOK, TOK), 1)
        score = jnp.where(((row ^ col) & 15) == 0, score, -1e30)
        e = jnp.exp(score - jnp.max(score, axis=-1, keepdims=True))
        pr = e / jnp.sum(e, axis=-1, keepdims=True)
        prob[h] = pr
        out = dot(pr.astype(BF16), head(vb, h))
        ao[:, pl.ds(pl.multiple_of(h * HDIM, HDIM), HDIM)] = out.astype(BF16)
        return 0

    lax.fori_loop(0, HEADS, forward, 0)
    for g in range(2):
        for p in range(3):
            aot[p, g] = dot(em[p], ao[:, g * NAT : (g + 1) * NAT], NT).astype(BF16)

    own_col = pl.ds(pl.multiple_of(c * HD, HD), HD)
    twin_col = pl.ds(pl.multiple_of((1 - c) * HD, HD), HD)
    twin = dev(x, y, z, (c + 1) % 2)
    for s in range(8):
        blk = cb.at[pl.ds(s * 4, 4), :, own_col]
        done(blk, a_rs.at[3, s])
        post(blk, blk, f_ss.at[s], f_rs.at[s], twin)
    for s in range(8):
        done(cb.at[pl.ds(s * 4, 4), :, twin_col], f_rs.at[s])

    def y_args(p, dy):
        to = (y + dy) % 4
        return (part.at[p, to], ry.at[p, y], y_ss.at[p, dy - 1], y_rs.at[p, y], dev(x, to, z, c))

    keep = (lax.broadcasted_iota(jnp.int32, (ROWS, 256), 0) & 15) < 12
    for p in range(3):
        def grad(i, _, p=p):
            g, t = i // 3, i % 3
            a = aot[p, g]
            lo = cb[:, :, pl.ds(pl.multiple_of(p * COL + t * 256, 256), 256)].reshape(TOK, 256)
            hi = cb[:, :, pl.ds(pl.multiple_of(3 * COL + t * 256, 256), 256)].reshape(TOK, 256)
            blk = jnp.where(keep, dot(a, lo), dot(a, hi)).astype(BF16)
            part[p, :, g, :, pl.ds(pl.multiple_of(t * 256, 256), 256)] = blk.reshape(4, 128, 256)
            return 0

        lax.fori_loop(0, 6, grad, 0)
        for dy in (2, 1, 3):
            post(*y_args(p, dy))

    for dy in range(1, 4):
        for zz in range(4):
            yy = (y + dy) % 4
            done(wp.at[:, yy, zz], w3_rs.at[yy * 4 + zz])

    def unpack(i, _):
        g, t = i // 3, i % 3
        rows = pl.ds(pl.multiple_of(g * NAT, NAT), NAT)
        rest = jnp.zeros((NAT, 256), F32)
        for p in range(3):
            blk = wp[g, :, :, :, pl.ds(pl.multiple_of(p * COL + t * 256, 256), 256)].reshape(ROWS, 256)
            wn[rows, pl.ds(pl.multiple_of(p * COL + t * 256, 256), 256)] = dot(um[0], blk).astype(BF16)
            rest += dot(um[p + 1], blk)
        wn[rows, pl.ds(pl.multiple_of(3 * COL + t * 256, 256), 256)] = rest.astype(BF16)
        return 0

    lax.fori_loop(0, 6, unpack, 0)

    def d_out(i, _):
        cols = pl.ds(pl.multiple_of(i * 256, 256), 256)
        dob[:, cols] = dot(cb[...].reshape(TOK, D), wn[cols, :], NT).astype(BF16)
        return 0

    lax.fori_loop(0, 3, d_out, 0)

    def backward(h, _):
        cols = pl.ds(pl.multiple_of(h * HDIM, HDIM), HDIM)
        do = dob[:, cols]
        pr = prob[h]
        gvb[:, :, cols] = dot(pr.astype(BF16), do, TN).astype(BF16).reshape(FRAMES, POS, HDIM)
        dpr = dot(do, head(vb, h), NT)
        ds = (pr * (dpr - jnp.sum(pr * dpr, axis=-1, keepdims=True))).astype(BF16)
        gqb[:, :, cols] = (dot(ds, head(kb, h)) * scale).astype(BF16).reshape(FRAMES, POS, HDIM)
        gkb[:, :, cols] = (dot(ds, head(qb, h), TN) * scale).astype(BF16).reshape(FRAMES, POS, HDIM)
        return 0

    lax.fori_loop(0, HEADS, backward, 0)

    def g_args(arr, dx, kz):
        px, pz = (x + dx) % 4, (zl + kz) % 2
        src = (gqb, gkb, gvb)[arr].at[pl.ds(pl.multiple_of((px * 2 + pz) * 4, 4), 4)]
        dst = (gq_out, gk_out, gv_out)[arr].at[
            :, pl.ds(pl.multiple_of(x * 16, 16), 16), pl.ds(pl.multiple_of(c * HALF, HALF), HALF)
        ]
        return src, dst, g_ss.at[arr, dx * 2 + kz], g_rs.at[arr, x * 2 + c], dev(px, y, zh * 2 + pz, zl)

    def g_each(fn):
        for arr in range(3):
            for dx in (2, 1, 3, 0):
                for kz in range(2):
                    fn(arr, dx, kz, a_own if dx == 0 and kz == 0 else None)

    g_each(lambda arr, dx, kz, own: post(*g_args(arr, dx, kz), own=own))

    def z_args(p, dz):
        to = (z + dz) % 4
        src = s1.at[p, :, pl.ds(pl.multiple_of(to * 32, 32), 32), :]
        return (src, rz.at[p, z], z_ss.at[p, dz - 1], z_rs.at[p, z], dev(x, y, to, c))

    for p in range(3):
        for dy in range(1, 4):
            yy = (y + dy) % 4
            done(ry.at[p, yy], y_rs.at[p, yy])
        total = part[p, y].astype(F32)
        for dy in range(1, 4):
            total += ry[p, (y + dy) % 4].astype(F32)
        s1[p] = total.astype(BF16)
        for dz in (2, 1, 3):
            post(*z_args(p, dz))

    def x_args(p, i, kc):
        core = (c + kc) % 2
        src = s2.at[p, i, pl.ds(pl.multiple_of(core * 16, 16), 16), :]
        return (src, rf.at[p, x], x_ss.at[p, i * 2 + kc], x_rs.at[p, x], dev(c * 2 + i, y, z, core))

    def x_own(i, kc):
        return x == c * 2 + i if kc == 0 else None

    for p in range(3):
        for dz in range(1, 4):
            zz = (z + dz) % 4
            done(rz.at[p, zz], z_rs.at[p, zz])
        total = s1[p, :, pl.ds(pl.multiple_of(z * 32, 32), 32), :].astype(F32)
        for dz in range(1, 4):
            total += rz[p, (z + dz) % 4].astype(F32)
        s2[p] = total.astype(BF16)
        for i in range(2):
            for kc in range(2):
                post(*x_args(p, i, kc), own=x_own(i, kc))

    norm = 1.0 / math.sqrt(32768.0)
    for p in range(3):
        for i in range(4):
            done(rf.at[p, i], x_rs.at[p, i])
        total = rf[p, 0].astype(F32)
        for i in range(1, 4):
            total += rf[p, i].astype(F32)
        gw_out[:, p * COL : (p + 1) * COL] = total * norm

    for arr in range(3):
        for i in range(8):
            col = pl.ds((i % 2) * HALF, HALF)
            done((gq_out, gk_out, gv_out)[arr].at[:, pl.ds((i // 2) * 16, 16), col], g_rs.at[arr, i])
    g_each(lambda arr, dx, kz, own: sent(g_args(arr, dx, kz)[0], g_ss.at[arr, dx * 2 + kz], own))
    a_each(lambda arr, dx, kc, own: sent(a_args(arr, dx, kc)[0], a_ss.at[arr, dx * 2 + kc], own))
    for dx in range(4):
        sent(w_in, w1_ss.at[dx], w_own if dx == 0 else None)
    for dz in range(1, 4):
        sent(w2_args(dz)[0], w2_ss.at[dz - 1])
    for dz in range(4):
        for dy in range(1, 4):
            sent(w3_args(dz, dy)[0], w3_ss.at[dz * 3 + dy - 1])
    for s in range(8):
        sent(cb.at[pl.ds(s * 4, 4), :, own_col], f_ss.at[s])
    for p in range(3):
        for d in range(1, 4):
            sent(y_args(p, d)[0], y_ss.at[p, d - 1])
            sent(z_args(p, d)[0], z_ss.at[p, d - 1])
        for i in range(2):
            for kc in range(2):
                sent(x_args(p, i, kc)[0], x_ss.at[p, i * 2 + kc], x_own(i, kc))


def local(query_in, key_in, value_in, cotangent, out_weight):
    top, rest = out_weight[:, :PK], out_weight[:, PK:]
    tail = rest.reshape(3, 4, COL).transpose(1, 0, 2).reshape(4, PK)
    w_packed = jnp.concatenate([top, tail], axis=0)
    any_spec = pl.BlockSpec(memory_space=pl.ANY)
    vmem_spec = pl.BlockSpec(memory_space=pltpu.VMEM)
    dma = pltpu.SemaphoreType.DMA
    act = jax.ShapeDtypeStruct((4, 64, HD), BF16)
    tok = (FRAMES, POS, HALF)
    gq, gk, gv, gw = pl.pallas_call(
        kernel,
        out_shape=(act, act, act, jax.ShapeDtypeStruct((16, PK), F32)),
        in_specs=[any_spec] * 4 + [vmem_spec],
        out_specs=(any_spec, any_spec, any_spec, vmem_spec),
        scratch_shapes=[
            pltpu.VMEM(tok, BF16), pltpu.VMEM(tok, BF16), pltpu.VMEM(tok, BF16),
            pltpu.VMEM((FRAMES, POS, D), BF16),
            pltpu.VMEM((2, 4, 4, 32, PK), BF16),
            pltpu.VMEM((HALF, D), BF16),
            pltpu.VMEM((HEADS, TOK, TOK), F32),
            pltpu.VMEM((TOK, HALF), BF16),
            pltpu.VMEM((3, 2, ROWS, TOK), BF16),
            pltpu.VMEM((3, ROWS, NAT), BF16),
            pltpu.VMEM((4, NAT, ROWS), BF16),
            pltpu.VMEM((3, 4, 2, 128, COL), BF16),
            pltpu.VMEM((3, 4, 2, 128, COL), BF16),
            pltpu.VMEM((3, 2, 128, COL), BF16),
            pltpu.VMEM((3, 4, 2, 32, COL), BF16),
            pltpu.VMEM((3, 2, 32, COL), BF16),
            pltpu.VMEM((3, 4, 16, COL), BF16),
            pltpu.VMEM((TOK, HALF), BF16),
            pltpu.VMEM(tok, BF16), pltpu.VMEM(tok, BF16), pltpu.VMEM(tok, BF16),
            dma((4, 8)), dma((4, 8)), dma((8,)), dma((8,)),
            dma((4,)), dma((4,)), dma((3,)), dma((4,)), dma((12,)), dma((16,)),
            dma((3, 3)), dma((3, 4)), dma((3, 3)), dma((3, 4)), dma((3, 4)), dma((3, 4)),
            dma((3, 8)), dma((3, 8)),
        ],
        compiler_params=pltpu.CompilerParams(
            collective_id=0, has_side_effects=True, vmem_limit_bytes=58 * 2**20
        ),
    )(
        query_in.reshape(4, 64, HD), key_in.reshape(4, 64, HD), value_in.reshape(4, 64, HD),
        cotangent.reshape(4, 64, D), w_packed,
    )
    tail = gw[12:].reshape(4, 3, COL).transpose(1, 0, 2).reshape(12, COL)
    grad_weight = jnp.concatenate([gw[:12], tail], axis=1)
    shape = (1, 4, 64, HD)
    return gq.reshape(shape), gk.reshape(shape), gv.reshape(shape), grad_weight


def solution(mesh):
    act, rows = P("dp", "seq", None, None), P(("seq", "dp"), None)
    return jax.shard_map(
        local, mesh=mesh, in_specs=(act, act, act, act, rows), out_specs=(act, act, act, rows),
        check_vma=False,
    )
```

time: 920 us -> 172 us (0.19)
  blocking collectives: 342 us -> 0 us
  starting transfers between devices: 205 us -> 0 us
  waiting for transfers between devices: 196 us -> 0 us
  Pallas kernels: 0 us -> 162 us
  local copies, waits for them, and re-layouts: 128 us -> 6.54 us
  matrix products: 23.4 us -> 0 us
  between operations: 14.9 us -> 0.66 us
    unnamed x1 -> x0, blocking collectives: 323 us -> none
    unnamed x32 -> x0, starting transfers between devices: 166 us -> none
    pallas_call x0 -> x1, Pallas kernels: none -> 162 us  [local(): pl.pallas_call(kernel, out_shape=(act, act, act, jax.ShapeDtypeStruct((16...]
    all_gather x1 -> x0, waiting for transfers between devices: 136 us -> none  [local(): lax.all_gather(out_weight, ('seq', 'dp'), axis=0, tiled=True)]
    unnamed x51 -> x7, local copies, waits for them, and re-layouts: 101 us -> 3.9 us
    all_to_all x7 -> x0, starting transfers between devices: 39.5 us -> none  [the longest x1 9.09 us: local(): lax.all_to_all(grad_key, 'seq', split_axis=1, concat_axis=2, tiled=True)]
    unnamed x33 -> x0, waiting for transfers between devices: 32.3 us -> none
    all_to_all x7 -> x0, waiting for transfers between devices: 27.3 us -> none  [the longest x1 9.45 us: local(): lax.all_to_all(key_in.reshape(head_shape), 'seq', split_axis=2, concat_ax...]
  transfers between devices with their start and end apart: 40 -> 0, of which waited for: 10 -> 0; matrix products, arithmetic and copies ran while one was open for 49% -> 0% of each run, Pallas kernels for 0% -> 0%
where the time goes in v1:
time: 172 us; the launch traced here: 171 us
  Pallas kernels  162 us (94%)
  local copies, waits for them, and re-layouts  6.54 us (4%)
  other arithmetic  2.26 us (1%)
    pallas_call x1, Pallas kernels, local(): pl.pallas_call(kernel, out_shape=(act, act, act, jax.ShapeDtypeStruct((16...  162 us
    unnamed x7, local copies, waits for them, and re-layouts  3.9 us

profile of v1, /device:TPU:3, one launch (start us, length us, event | category | flops | bytes accessed | tf_op | source)
XLA Modules:
  0.0 171.1 jit_solution(1723358316868488758)
XLA Ops:
  0.6 0.7 slice.13
  1.4 0.9 slice.12
  2.3 0.7 pad_maximum_fusion.1.w_in
  2.9 161.6 %shard_map.84 = (bf16[4,64,1536]{2,1,0:T(8,128)(2,1)}, bf16[4,64,1536]{2,1,0:T(8,128)(2,1)}, bf16[4,64,1536]{2,1,0:T(8,128)(2,1)}, f32[16,2304]{1,0:T(8,128)}) custom-call(bf16[4,64,1536]{2,1,0:T(8,128)(2,1)} %bitcast.18, bf16[4,64,1536]{2,1,0:T(8,128)(2,1)} %bitcast.19, bf16[4,64,1536]{2,1,0:T(8,128)(2,1)} %bitcast.20, bf16[4,64,3072]{2,1,0:T(8,128)(2,1)} %bitcast.14, ...), custom_call_target="tpu_custom_call" | custom-call | tf_op jit(solution)/shard_map/pallas_call | solution.py:344
  164.6 0.0 copy-start.1
  164.6 1.0 slice.15
  165.6 1.6 pad_maximum_fusion
  167.2 0.0 copy-start
  167.2 2.1 %copy.14 = bf16[1,4,64,1536]{3,2,1,0:T(8,128)(2,1)} copy(bf16[1,4,64,1536]{3,2,1,0:T(8,128)(2,1)} %bitcast.17) | data formatting | bytes 1572864
  169.3 0.0 copy-done.1
  169.3 0.9 copy.15
  170.2 0.0 copy-done
  170.2 0.9 copy.16
  (2 shorter events, 0.0 us)
Async XLA Ops:
  164.6 4.7 %copy-start.1 = (bf16[4,64,1536]{2,1,0:T(8,128)(2,1)S(1)}, bf16[4,64,1536]{2,1,0:T(8,128)(2,1)}, u32[]{:S(2)}) copy-start(bf16[4,64,1536]{2,1,0:T(8,128)(2,1)} %get-tuple-element.9) | copy-start | bytes 2359300
  167.2 3.0 %copy-start = (bf16[4,64,1536]{2,1,0:T(8,128)(2,1)S(1)}, bf16[4,64,1536]{2,1,0:T(8,128)(2,1)}, u32[]{:S(2)}) copy-start(bf16[4,64,1536]{2,1,0:T(8,128)(2,1)} %get-tuple-element.10) | copy-start | bytes 2359300

commit v2 on v1

v2 whole, which is shorter than its diff:
```python
import math

import jax
import jax.numpy as jnp
from jax import lax
from jax.experimental import pallas as pl
from jax.experimental.pallas import tpu as pltpu
from jax.sharding import PartitionSpec as P

MESH = pl.DeviceIdType.MESH
F32, BF16 = jnp.float32, jnp.bfloat16

FRAMES, POS, HD, D, HDIM = 32, 16, 1536, 3072, 128
HALF = HD // 2
TOK = FRAMES * POS
HEADS = HALF // HDIM
PK = 2304
COL = 768
ROWS = 512
NAT = 384
NT = (((1,), (1,)), ((), ()))
TN = (((0,), (0,)), ((), ()))


def dot(a, b, dims=(((1,), (0,)), ((), ()))):
    return lax.dot_general(a, b, dims, preferred_element_type=F32)


def kernel(
    q_in, k_in, v_in, c_in, w_in,
    gq_out, gk_out, gv_out, gw_out,
    qb, kb, vb, cb, wf, wpk, wp, wn, prob, ao, aot, em, um, part, rh, ry, s1, rzh, rz, s2, rf, dob, gqb, gkb, gvb,
    a_ss, a_rs, f_ss, f_rs, w1_ss, w1_rs, w2_ss, w2_rs, w3_ss, w3_rs,
    y_ss, y_rs, z_ss, z_rs, x_ss, x_rs, g_ss, g_rs,
):
    seq, dp = lax.axis_index("seq"), lax.axis_index("dp")
    x, zl = seq // 2, seq % 2
    zh, y, c = dp // 8, (dp // 2) % 4, dp % 2
    z = zh * 2 + zl

    def dev(x, y, z, c):
        return {"seq": x * 2 + z % 2, "dp": (z // 2) * 8 + y * 2 + c}

    def remote(src, dst, ss, rs, to):
        return pltpu.make_async_remote_copy(
            src_ref=src, dst_ref=dst, send_sem=ss, recv_sem=rs, device_id=to, device_id_type=MESH
        )

    def done(ref, sem):
        pltpu.make_async_copy(ref, ref, sem).wait()

    def post(src, dst, ss, rs, to, own=None):
        if own is None:
            remote(src, dst, ss, rs, to).start()
            return

        @pl.when(own)
        def _():
            pltpu.make_async_copy(src, dst, rs).start()

        @pl.when(jnp.logical_not(own))
        def _():
            remote(src, dst, ss, rs, to).start()

    def sent(src, ss, own=None):
        if own is None:
            done(src, ss)
        else:
            pl.when(jnp.logical_not(own))(lambda: done(src, ss))

    z1, z3 = zh * 2 + 1 - zl, 3 - z
    z2 = (z + 2) % 4
    up, down = (y + 1) % 4, (y + 3) % 4
    far = (y + 2) % 4

    barrier = pltpu.get_barrier_semaphore()
    peers = [
        dev((x + dx) % 4, y, zh * 2 + (zl + kz) % 2, (c + kc) % 2)
        for dx in range(4) for kz in range(2) for kc in range(2) if dx or kz or kc
    ]
    peers += [dev(x, y, z3, c), dev(x, up, z, c), dev(x, down, z, c)]
    for to in peers:
        pl.semaphore_signal(barrier, inc=1, device_id=to, device_id_type=MESH)

    rows = w_in[...].astype(F32)
    wf[0:12, :] = rows[:, :PK]
    for p in range(3):
        wf[12:16, p * COL : (p + 1) * COL] = rows[4 * p : 4 * p + 4, PK:]
    wpk[...] = wf[...].astype(BF16)
    pl.semaphore_wait(barrier, len(peers))

    half = x // 2
    w_own = c == half
    w_slot = wp.at[x % 2, y, z, pl.ds(pl.multiple_of(c * 16, 16), 16), :]

    def w1_args(dx):
        return (wpk, w_slot, w1_ss.at[dx], w1_rs.at[(x % 2) * 2 + c], dev((x + dx) % 4, y, z, half))

    for dx in (2, 1, 3, 0):
        post(*w1_args(dx), own=w_own if dx == 0 else None)

    mine = pl.ds(pl.multiple_of(seq * 4, 4), 4)
    cross = zl != c

    def cot_cols(core, part_no):
        other = core if part_no == 0 else 1 - core
        return pl.ds(pl.multiple_of(core * HD + other * COL, COL), COL)

    def a_args(arr, dx, kc):
        px, core = (x + dx) % 4, (c + kc) % 2
        to = dev(px, y, zh * 2 + c, core)
        pos = pl.ds(pl.multiple_of(px * 16, 16), 16)
        if arr < 3:
            col = pl.ds(pl.multiple_of(core * HALF, HALF), HALF)
            src = (q_in, k_in, v_in)[arr].at[:, pos, col]
            dst = (qb, kb, vb)[arr].at[mine]
        else:
            col = cot_cols(core, arr - 3)
            src = c_in.at[:, pos, col]
            dst = cb.at[mine, :, col]
        return src, dst, a_ss.at[arr, dx * 2 + kc], a_rs.at[arr, seq], to

    def a_post(arrs, crossing):
        @pl.when(cross if crossing else jnp.logical_not(cross))
        def _():
            for arr in arrs:
                for dx in (2, 1, 3, 0):
                    for kc in range(2):
                        src, dst, ss, rs, to = a_args(arr, dx, kc)
                        if not crossing and dx == 0 and kc == 0:
                            pltpu.make_async_copy(src, dst, rs).start()
                        else:
                            remote(src, dst, ss, rs, to).start()

    a_post((0, 1, 2), False)

    def packed(shape, axis):
        m = lax.broadcasted_iota(jnp.int32, shape, axis)
        j, r = m >> 4, m & 15
        owner = ((j >> 1) & 1) * 16 + ((j >> 2) & 1) * 8 + (j >> 3) * 2 + (j & 1)
        return owner * 12, r

    base, r = packed((ROWS, NAT), 0)
    n = lax.broadcasted_iota(jnp.int32, (ROWS, NAT), 1)
    for p in range(3):
        hit = n == jnp.where(r < 12, base + r, base + (r - 12 + 4 * p))
        em[p] = jnp.where(hit, 1.0, 0.0).astype(BF16)
    base, r = packed((NAT, ROWS), 1)
    n = lax.broadcasted_iota(jnp.int32, (NAT, ROWS), 0)
    um[0] = jnp.where(n == jnp.where(r < 12, base + r, -1), 1.0, 0.0).astype(BF16)
    for p in range(3):
        hit = n == jnp.where(r < 12, -1, base + (r - 12 + 4 * p))
        um[p + 1] = jnp.where(hit, 1.0, 0.0).astype(BF16)

    w_z = (z, z3, z1, z2)

    def w2_args(i):
        blk = wp.at[:, y, z] if i < 2 else wp.at[:, y, z1]
        return (blk, blk, w2_ss.at[i], w2_rs.at[i], dev(x, y, z1 if i == 0 else z3, c))

    def w3_args(i, k):
        zz = w_z[i]
        blk = (wp.at[:, y, zz], wp.at[:, y, zz], wp.at[0, down, zz], wp.at[1, up, zz])[k]
        to = dev(x, down if k % 2 else up, z, c)
        return (blk, blk, w3_ss.at[i, k], w3_rs.at[i, k], to)

    def w3_post(i):
        post(*w3_args(i, 0))
        post(*w3_args(i, 1))

    def w3_relay(i):
        done(wp.at[:, down, w_z[i]], w3_rs.at[i, 0])
        post(*w3_args(i, 2))
        done(wp.at[:, up, w_z[i]], w3_rs.at[i, 1])
        post(*w3_args(i, 3))

    for i in range(4):
        done(wp.at[i // 2, y, z, pl.ds((i % 2) * 16, 16), :], w1_rs.at[i])
    post(*w2_args(0))
    post(*w2_args(1))
    w3_post(0)
    a_post((0,), True)
    done(wp.at[:, y, z3], w2_rs.at[1])
    w3_post(1)
    w3_relay(0)
    done(wp.at[:, y, z1], w2_rs.at[0])
    post(*w2_args(2))
    w3_post(2)
    a_post((1, 2), True)
    a_post((3,), False)
    w3_relay(1)
    done(wp.at[:, y, z2], w2_rs.at[2])
    w3_post(3)
    a_post((3,), True)
    a_post((4,), False)
    w3_relay(2)
    a_post((4,), True)
    w3_relay(3)

    for s in range(8):
        for arr, buf in enumerate((qb, kb, vb)):
            done(buf.at[pl.ds(s * 4, 4)], a_rs.at[arr, s])

    scale = 1.0 / math.sqrt(HDIM)

    def head(buf, h):
        return buf[:, :, pl.ds(pl.multiple_of(h * HDIM, HDIM), HDIM)].reshape(TOK, HDIM)

    def forward(h, _):
        score = dot(head(qb, h), head(kb, h), NT) * scale
        row = lax.broadcasted_iota(jnp.int32, (TOK, TOK), 0)
        col = lax.broadcasted_iota(jnp.int32, (TOK, TOK), 1)
        score = jnp.where(((row ^ col) & 15) == 0, score, -1e30)
        e = jnp.exp(score - jnp.max(score, axis=-1, keepdims=True))
        pr = e / jnp.sum(e, axis=-1, keepdims=True)
        prob[h] = pr
        out = dot(pr.astype(BF16), head(vb, h))
        ao[:, pl.ds(pl.multiple_of(h * HDIM, HDIM), HDIM)] = out.astype(BF16)
        return 0

    lax.fori_loop(0, HEADS, forward, 0)
    for g in range(2):
        for p in range(3):
            aot[p, g] = dot(em[p], ao[:, g * NAT : (g + 1) * NAT], NT).astype(BF16)

    for i in range(4):
        done(wp.at[0, far, w_z[i]], w3_rs.at[i, 2])
        done(wp.at[1, far, w_z[i]], w3_rs.at[i, 3])

    def unpack(i, _):
        g, t = i // 3, i % 3
        rows = pl.ds(pl.multiple_of(g * NAT, NAT), NAT)
        rest = jnp.zeros((NAT, 256), F32)
        for p in range(3):
            blk = wp[g, :, :, :, pl.ds(pl.multiple_of(p * COL + t * 256, 256), 256)].reshape(ROWS, 256)
            wn[rows, pl.ds(pl.multiple_of(p * COL + t * 256, 256), 256)] = dot(um[0], blk).astype(BF16)
            rest += dot(um[p + 1], blk)
        wn[rows, pl.ds(pl.multiple_of(3 * COL + t * 256, 256), 256)] = rest.astype(BF16)
        return 0

    lax.fori_loop(0, 6, unpack, 0)

    twin = dev(x, y, z, (c + 1) % 2)

    def pass_on(k):
        for s in range(8):
            blk = cb.at[pl.ds(s * 4, 4), :, cot_cols(c, k)]
            done(blk, a_rs.at[3 + k, s])
            post(blk, blk, f_ss.at[k, s], f_rs.at[k, s], twin)

    def passed(k):
        for s in range(8):
            done(cb.at[pl.ds(s * 4, 4), :, cot_cols(1 - c, k)], f_rs.at[k, s])

    def y_args(p, k):
        src, dst = (
            (part.at[p, far, 0], rh.at[p, 0]), (part.at[p, far, 1], rh.at[p, 1]),
            (part.at[p, up, 1], ry.at[p, 0, 1]), (part.at[p, down, 0], ry.at[p, 1, 0]),
            (part.at[p, up, 0], ry.at[p, 0, 0]), (part.at[p, down, 1], ry.at[p, 1, 1]),
        )[k]
        return (src, dst, y_ss.at[p, k], y_rs.at[p, k], dev(x, down if k % 2 else up, z, c))

    def y_relay(p):
        for k, (to, i) in enumerate(((up, 0), (down, 1))):
            done(rh.at[p, k], y_rs.at[p, k])
            part[p, to, i] = (part[p, to, i].astype(F32) + rh[p, k].astype(F32)).astype(BF16)
            post(*y_args(p, k + 4))

    pass_on(0)
    passed(0)

    keep = (lax.broadcasted_iota(jnp.int32, (ROWS, 256), 0) & 15) < 12
    for p in range(3):
        def grad(i, _, p=p):
            g, t = i // 3, i % 3
            a = aot[p, g]
            lo = cb[:, :, pl.ds(pl.multiple_of(p * COL + t * 256, 256), 256)].reshape(TOK, 256)
            hi = cb[:, :, pl.ds(pl.multiple_of(3 * COL + t * 256, 256), 256)].reshape(TOK, 256)
            blk = jnp.where(keep, dot(a, lo), dot(a, hi)).astype(BF16)
            part[p, :, g, :, pl.ds(pl.multiple_of(t * 256, 256), 256)] = blk.reshape(4, 128, 256)
            return 0

        lax.fori_loop(0, 6, grad, 0)
        for k in range(4):
            post(*y_args(p, k))
        if p == 0:
            pass_on(1)
            passed(1)

    def d_out(i, _):
        cols = pl.ds(pl.multiple_of(i * 256, 256), 256)
        dob[:, cols] = dot(cb[...].reshape(TOK, D), wn[cols, :], NT).astype(BF16)
        return 0

    lax.fori_loop(0, 3, d_out, 0)

    def backward(h, _):
        cols = pl.ds(pl.multiple_of(h * HDIM, HDIM), HDIM)
        do = dob[:, cols]
        pr = prob[h]
        gvb[:, :, cols] = dot(pr.astype(BF16), do, TN).astype(BF16).reshape(FRAMES, POS, HDIM)
        dpr = dot(do, head(vb, h), NT)
        ds = (pr * (dpr - jnp.sum(pr * dpr, axis=-1, keepdims=True))).astype(BF16)
        gqb[:, :, cols] = (dot(ds, head(kb, h)) * scale).astype(BF16).reshape(FRAMES, POS, HDIM)
        gkb[:, :, cols] = (dot(ds, head(qb, h), TN) * scale).astype(BF16).reshape(FRAMES, POS, HDIM)
        return 0

    y_relay(0)
    lax.fori_loop(0, HEADS, backward, 0)

    def g_args(arr, dx, kz):
        px, pz = (x + dx) % 4, (zl + kz) % 2
        src = (gqb, gkb, gvb)[arr].at[pl.ds(pl.multiple_of((px * 2 + pz) * 4, 4), 4)]
        dst = (gq_out, gk_out, gv_out)[arr].at[
            :, pl.ds(pl.multiple_of(x * 16, 16), 16), pl.ds(pl.multiple_of(c * HALF, HALF), HALF)
        ]
        return src, dst, g_ss.at[arr, dx * 2 + kz], g_rs.at[arr, x * 2 + c], dev(px, y, zh * 2 + pz, zl)

    a_own = zl == c

    def g_each(fn):
        for arr in range(3):
            for dx in (2, 1, 3, 0):
                for kz in (1, 0):
                    fn(arr, dx, kz, a_own if dx == 0 and kz == 0 else None)

    g_each(lambda arr, dx, kz, own: post(*g_args(arr, dx, kz), own=own))
    y_relay(1)
    y_relay(2)

    def s1_rows(zz):
        return pl.ds(pl.multiple_of(zz * 32, 32), 32)

    def z_args(p, k):
        src = s1.at[p, :, s1_rows((z2, z3, z1)[k]), :]
        dst = (rzh.at[p], rz.at[p, 0], rz.at[p, 1])[k]
        return (src, dst, z_ss.at[p, k], z_rs.at[p, k], dev(x, y, z1 if k == 2 else z3, c))

    def y_sum(p):
        total = part[p, y].astype(F32)
        for k, dst in ((2, ry.at[p, 0, 1]), (3, ry.at[p, 1, 0]), (4, ry.at[p, 0, 0]), (5, ry.at[p, 1, 1])):
            done(dst, y_rs.at[p, k])
        s1[p] = (total + ry[p, 0].astype(F32) + ry[p, 1].astype(F32)).astype(BF16)
        post(*z_args(p, 0))
        post(*z_args(p, 1))

    def z_relay(p):
        done(rzh.at[p], z_rs.at[p, 0])
        rows = s1_rows(z1)
        s1[p, :, rows, :] = (s1[p, :, rows, :].astype(F32) + rzh[p].astype(F32)).astype(BF16)
        post(*z_args(p, 2))

    def x_args(p, i, kc):
        core = (c + kc) % 2
        src = s2.at[p, i, pl.ds(pl.multiple_of(core * 16, 16), 16), :]
        return (src, rf.at[p, x], x_ss.at[p, i * 2 + kc], x_rs.at[p, x], dev(c * 2 + i, y, z, core))

    def x_own(i, kc):
        return x == c * 2 + i if kc == 0 else None

    def z_sum(p):
        for k in range(2):
            done(rz.at[p, k], z_rs.at[p, k + 1])
        total = s1[p, :, s1_rows(z), :].astype(F32)
        s2[p] = (total + rz[p, 0].astype(F32) + rz[p, 1].astype(F32)).astype(BF16)
        for i in range(2):
            for kc in range(2):
                post(*x_args(p, i, kc), own=x_own(i, kc))

    y_sum(0)
    y_sum(1)
    z_relay(0)
    y_sum(2)
    z_relay(1)
    z_sum(0)
    z_relay(2)
    z_sum(1)
    z_sum(2)

    norm = 1.0 / math.sqrt(32768.0)
    for p in range(3):
        for i in range(4):
            done(rf.at[p, i], x_rs.at[p, i])
        total = rf[p, 0].astype(F32)
        for i in range(1, 4):
            total += rf[p, i].astype(F32)
        total *= norm
        gw_out[:, p * COL : (p + 1) * COL] = total[:12]
        gw_out[4 * p : 4 * p + 4, PK:] = total[12:]

    for arr in range(3):
        for i in range(8):
            col = pl.ds((i % 2) * HALF, HALF)
            done((gq_out, gk_out, gv_out)[arr].at[:, pl.ds((i // 2) * 16, 16), col], g_rs.at[arr, i])
    g_each(lambda arr, dx, kz, own: sent(g_args(arr, dx, kz)[0], g_ss.at[arr, dx * 2 + kz], own))
    for arr in range(5):
        for dx in range(4):
            for kc in range(2):
                own = a_own if dx == 0 and kc == 0 else None
                sent(a_args(arr, dx, kc)[0], a_ss.at[arr, dx * 2 + kc], own)
    for dx in range(4):
        sent(wpk, w1_ss.at[dx], w_own if dx == 0 else None)
    for i in range(3):
        sent(w2_args(i)[0], w2_ss.at[i])
    for i in range(4):
        for k in range(4):
            sent(w3_args(i, k)[0], w3_ss.at[i, k])
    for k in range(2):
        for s in range(8):
            sent(cb.at[pl.ds(s * 4, 4), :, cot_cols(c, k)], f_ss.at[k, s])
    for p in range(3):
        for k in range(6):
            sent(y_args(p, k)[0], y_ss.at[p, k])
        for k in range(3):
            sent(z_args(p, k)[0], z_ss.at[p, k])
        for i in range(2):
            for kc in range(2):
                sent(x_args(p, i, kc)[0], x_ss.at[p, i * 2 + kc], x_own(i, kc))


def local(query_in, key_in, value_in, cotangent, out_weight):
    any_spec = pl.BlockSpec(memory_space=pl.ANY)
    vmem_spec = pl.BlockSpec(memory_space=pltpu.VMEM)
    dma = pltpu.SemaphoreType.DMA
    act = jax.ShapeDtypeStruct((4, 64, HD), BF16)
    tok = (FRAMES, POS, HALF)
    gq, gk, gv, gw = pl.pallas_call(
        kernel,
        out_shape=(act, act, act, jax.ShapeDtypeStruct((12, D), F32)),
        in_specs=[any_spec] * 4 + [vmem_spec],
        out_specs=(any_spec, any_spec, any_spec, vmem_spec),
        scratch_shapes=[
            pltpu.VMEM(tok, BF16), pltpu.VMEM(tok, BF16), pltpu.VMEM(tok, BF16),
            pltpu.VMEM((FRAMES, POS, D), BF16),
            pltpu.VMEM((16, PK), F32),
            pltpu.VMEM((16, PK), BF16),
            pltpu.VMEM((2, 4, 4, 32, PK), BF16),
            pltpu.VMEM((HALF, D), BF16),
            pltpu.VMEM((HEADS, TOK, TOK), F32),
            pltpu.VMEM((TOK, HALF), BF16),
            pltpu.VMEM((3, 2, ROWS, TOK), BF16),
            pltpu.VMEM((3, ROWS, NAT), BF16),
            pltpu.VMEM((4, NAT, ROWS), BF16),
            pltpu.VMEM((3, 4, 2, 128, COL), BF16),
            pltpu.VMEM((3, 2, 128, COL), BF16),
            pltpu.VMEM((3, 2, 2, 128, COL), BF16),
            pltpu.VMEM((3, 2, 128, COL), BF16),
            pltpu.VMEM((3, 2, 32, COL), BF16),
            pltpu.VMEM((3, 2, 2, 32, COL), BF16),
            pltpu.VMEM((3, 2, 32, COL), BF16),
            pltpu.VMEM((3, 4, 16, COL), BF16),
            pltpu.VMEM((TOK, HALF), BF16),
            pltpu.VMEM(tok, BF16), pltpu.VMEM(tok, BF16), pltpu.VMEM(tok, BF16),
            dma((5, 8)), dma((5, 8)), dma((2, 8)), dma((2, 8)),
            dma((4,)), dma((4,)), dma((3,)), dma((3,)), dma((4, 4)), dma((4, 4)),
            dma((3, 6)), dma((3, 6)), dma((3, 3)), dma((3, 3)), dma((3, 4)), dma((3, 4)),
            dma((3, 8)), dma((3, 8)),
        ],
        compiler_params=pltpu.CompilerParams(
            collective_id=0, has_side_effects=True, vmem_limit_bytes=58 * 2**20
        ),
    )(
        query_in.reshape(4, 64, HD), key_in.reshape(4, 64, HD), value_in.reshape(4, 64, HD),
        cotangent.reshape(4, 64, D), out_weight,
    )
    shape = (1, 4, 64, HD)
    return gq.reshape(shape), gk.reshape(shape), gv.reshape(shape), gw


def solution(mesh):
    act, rows = P("dp", "seq", None, None), P(("seq", "dp"), None)
    return jax.shard_map(
        local, mesh=mesh, in_specs=(act, act, act, act, rows), out_specs=(act, act, act, rows),
        check_vma=False,
    )
```

time: 172 us -> 141 us (0.82)
  the two profiles are of different devices: /device:TPU:3 before, /device:TPU:1 now
where the time goes in v2:
time: 141 us
  Pallas kernels  136 us (96%)
  local copies, waits for them, and re-layouts  4.63 us (3%)
    pallas_call x1, Pallas kernels, local(): pl.pallas_call(kernel, out_shape=(act, act, act, jax.ShapeDtypeStruct((12...  136 us
    unnamed x10, local copies, waits for them, and re-layouts  4.63 us

profile of v2, /device:TPU:1, one launch (start us, length us, event | category | flops | bytes accessed | tf_op | source)
XLA Modules:
  0.0 141.2 jit_solution(13312939577970708532)
XLA Ops:
  0.6 135.9 %shard_map.84 = (bf16[4,64,1536]{2,1,0:T(8,128)(2,1)}, bf16[4,64,1536]{2,1,0:T(8,128)(2,1)}, bf16[4,64,1536]{2,1,0:T(8,128)(2,1)}, f32[12,3072]{1,0:T(8,128)}) custom-call(bf16[4,64,1536]{2,1,0:T(8,128)(2,1)} %bitcast.11, bf16[4,64,1536]{2,1,0:T(8,128)(2,1)} %bitcast.12, bf16[4,64,1536]{2,1,0:T(8,128)(2,1)} %bitcast.13, bf16[4,64,3072]{2,1,0:T(8,128)(2,1)} %bitcast.7, ...), custom_call_target="tpu_custom_call" | custom-call | tf_op jit(solution)/shard_map/pallas_call | solution.py:427
  136.5 0.0 copy-start.1
  136.5 0.0 copy-start
  136.5 2.2 %copy.13 = bf16[1,4,64,1536]{3,2,1,0:T(8,128)(2,1)} copy(bf16[1,4,64,1536]{3,2,1,0:T(8,128)(2,1)} %bitcast.10) | data formatting | bytes 1572864
  138.7 0.0 copy-done.1
  138.7 0.0 copy-start.2
  138.7 0.9 copy.14
  139.6 0.0 copy-done
  139.6 0.9 copy.15
  140.5 0.0 copy-done.2
  140.5 0.7 copy.16
Async XLA Ops:
  136.5 2.2 %copy-start.1 = (bf16[4,64,1536]{2,1,0:T(8,128)(2,1)S(1)}, bf16[4,64,1536]{2,1,0:T(8,128)(2,1)}, u32[]{:S(2)}) copy-start(bf16[4,64,1536]{2,1,0:T(8,128)(2,1)} %get-tuple-element.9) | copy-start | bytes 2359300
  136.5 3.1 %copy-start = (bf16[4,64,1536]{2,1,0:T(8,128)(2,1)S(1)}, bf16[4,64,1536]{2,1,0:T(8,128)(2,1)}, u32[]{:S(2)}) copy-start(bf16[4,64,1536]{2,1,0:T(8,128)(2,1)} %get-tuple-element.10) | copy-start | bytes 2359300
  138.7 1.8 %copy-start.2 = (f32[12,3072]{1,0:T(8,128)S(1)}, f32[12,3072]{1,0:T(8,128)}, u32[]{:S(2)}) copy-start(f32[12,3072]{1,0:T(8,128)} %get-tuple-element.19) | copy-start | bytes 442372

commit v3 on v2

--- a/solution.py
+++ b/solution.py
@@ -110,14 +110,15 @@
         px, core = (x + dx) % 4, (c + kc) % 2
         to = dev(px, y, zh * 2 + c, core)
         pos = pl.ds(pl.multiple_of(px * 16, 16), 16)
-        if arr < 3:
-            col = pl.ds(pl.multiple_of(core * HALF, HALF), HALF)
-            src = (q_in, k_in, v_in)[arr].at[:, pos, col]
-            dst = (qb, kb, vb)[arr].at[mine]
-        else:
-            col = cot_cols(core, arr - 3)
+        if arr < 2:
+            col = cot_cols(core, arr)
             src = c_in.at[:, pos, col]
             dst = cb.at[mine, :, col]
+        else:
+            g, i = (arr - 2) // 3, (arr - 2) % 3
+            col = pl.ds(pl.multiple_of(core * HALF + g * NAT, NAT), NAT)
+            src = (q_in, k_in, v_in)[i].at[:, pos, col]
+            dst = (qb, kb, vb)[i].at[mine, :, pl.ds(g * NAT, NAT)]
         return src, dst, a_ss.at[arr, dx * 2 + kc], a_rs.at[arr, seq], to
 
     def a_post(arrs, crossing):
@@ -132,7 +133,13 @@
                         else:
                             remote(src, dst, ss, rs, to).start()
 
-    a_post((0, 1, 2), False)
+    def a_sent(arrs):
+        for arr in arrs:
+            for dx in (2, 1, 3, 0):
+                for kc in range(2):
+                    sent(a_args(arr, dx, kc)[0], a_ss.at[arr, dx * 2 + kc], zl == c if dx == 0 and kc == 0 else None)
+
+    a_post((0, 1), False)
 
     def packed(shape, axis):
         m = lax.broadcasted_iota(jnp.int32, shape, axis)
@@ -173,6 +180,18 @@
         post(*w3_args(i, 2))
         done(wp.at[:, up, w_z[i]], w3_rs.at[i, 1])
         post(*w3_args(i, 3))
+
+    twin = dev(x, y, z, (c + 1) % 2)
+
+    def pass_on(k):
+        for s in range(8):
+            blk = cb.at[pl.ds(s * 4, 4), :, cot_cols(c, k)]
+            done(blk, a_rs.at[k, s])
+            post(blk, blk, f_ss.at[k, s], f_rs.at[k, s], twin)
+
+    def passed(k):
+        for s in range(8):
+            done(cb.at[pl.ds(s * 4, 4), :, cot_cols(1 - c, k)], f_rs.at[k, s])
 
     for i in range(4):
         done(wp.at[i // 2, y, z, pl.ds((i % 2) * 16, 16), :], w1_rs.at[i])
@@ -186,20 +205,25 @@
     done(wp.at[:, y, z1], w2_rs.at[0])
     post(*w2_args(2))
     w3_post(2)
-    a_post((1, 2), True)
-    a_post((3,), False)
+    a_post((1,), True)
+    a_post((2, 3, 4), False)
+    a_sent((0,))
+    a_post((2, 3, 4), True)
     w3_relay(1)
+    pass_on(0)
     done(wp.at[:, y, z2], w2_rs.at[2])
     w3_post(3)
-    a_post((3,), True)
-    a_post((4,), False)
     w3_relay(2)
-    a_post((4,), True)
+    a_sent((2, 3, 4))
+    a_post((5, 6, 7), False)
+    a_post((5, 6, 7), True)
+    pass_on(1)
     w3_relay(3)
 
-    for s in range(8):
-        for arr, buf in enumerate((qb, kb, vb)):
-            done(buf.at[pl.ds(s * 4, 4)], a_rs.at[arr, s])
+    def attn_ready(g):
+        for s in range(8):
+            for i, buf in enumerate((qb, kb, vb)):
+                done(buf.at[pl.ds(s * 4, 4), :, pl.ds(g * NAT, NAT)], a_rs.at[2 + 3 * g + i, s])
 
     scale = 1.0 / math.sqrt(HDIM)
 
@@ -218,15 +242,6 @@
         ao[:, pl.ds(pl.multiple_of(h * HDIM, HDIM), HDIM)] = out.astype(BF16)
         return 0
 
-    lax.fori_loop(0, HEADS, forward, 0)
-    for g in range(2):
-        for p in range(3):
-            aot[p, g] = dot(em[p], ao[:, g * NAT : (g + 1) * NAT], NT).astype(BF16)
-
-    for i in range(4):
-        done(wp.at[0, far, w_z[i]], w3_rs.at[i, 2])
-        done(wp.at[1, far, w_z[i]], w3_rs.at[i, 3])
-
     def unpack(i, _):
         g, t = i // 3, i % 3
         rows = pl.ds(pl.multiple_of(g * NAT, NAT), NAT)
@@ -238,61 +253,56 @@
         wn[rows, pl.ds(pl.multiple_of(3 * COL + t * 256, 256), 256)] = rest.astype(BF16)
         return 0
 
-    lax.fori_loop(0, 6, unpack, 0)
-
-    twin = dev(x, y, z, (c + 1) % 2)
-
-    def pass_on(k):
-        for s in range(8):
-            blk = cb.at[pl.ds(s * 4, 4), :, cot_cols(c, k)]
-            done(blk, a_rs.at[3 + k, s])
-            post(blk, blk, f_ss.at[k, s], f_rs.at[k, s], twin)
-
-    def passed(k):
-        for s in range(8):
-            done(cb.at[pl.ds(s * 4, 4), :, cot_cols(1 - c, k)], f_rs.at[k, s])
-
-    def y_args(p, k):
-        src, dst = (
-            (part.at[p, far, 0], rh.at[p, 0]), (part.at[p, far, 1], rh.at[p, 1]),
-            (part.at[p, up, 1], ry.at[p, 0, 1]), (part.at[p, down, 0], ry.at[p, 1, 0]),
-            (part.at[p, up, 0], ry.at[p, 0, 0]), (part.at[p, down, 1], ry.at[p, 1, 1]),
-        )[k]
-        return (src, dst, y_ss.at[p, k], y_rs.at[p, k], dev(x, down if k % 2 else up, z, c))
-
-    def y_relay(p):
-        for k, (to, i) in enumerate(((up, 0), (down, 1))):
-            done(rh.at[p, k], y_rs.at[p, k])
-            part[p, to, i] = (part[p, to, i].astype(F32) + rh[p, k].astype(F32)).astype(BF16)
-            post(*y_args(p, k + 4))
-
-    pass_on(0)
-    passed(0)
-
     keep = (lax.broadcasted_iota(jnp.int32, (ROWS, 256), 0) & 15) < 12
-    for p in range(3):
-        def grad(i, _, p=p):
-            g, t = i // 3, i % 3
+
+    def grad(g, p):
+        st = g * 3 + p
+
+        def tile(t, _):
             a = aot[p, g]
+            cols = pl.ds(pl.multiple_of(t * 256, 256), 256)
             lo = cb[:, :, pl.ds(pl.multiple_of(p * COL + t * 256, 256), 256)].reshape(TOK, 256)
             hi = cb[:, :, pl.ds(pl.multiple_of(3 * COL + t * 256, 256), 256)].reshape(TOK, 256)
             blk = jnp.where(keep, dot(a, lo), dot(a, hi)).astype(BF16)
-            part[p, :, g, :, pl.ds(pl.multiple_of(t * 256, 256), 256)] = blk.reshape(4, 128, 256)
+            part[st, :, :, cols] = blk.reshape(4, 128, 256)
             return 0
 
-        lax.fori_loop(0, 6, grad, 0)
+        lax.fori_loop(0, 3, tile, 0)
         for k in range(4):
-            post(*y_args(p, k))
-        if p == 0:
-            pass_on(1)
+            post(*y_args(st, k))
+
+    lo, hi = pl.ds(0, 64), pl.ds(64, 64)
+
+    def y_args(st, k):
+        src, dst = (
+            (part.at[st, far, lo], rh.at[st, 0]), (part.at[st, far, hi], rh.at[st, 1]),
+            (part.at[st, up, hi], ry.at[st, 0, hi]), (part.at[st, down, lo], ry.at[st, 1, lo]),
+            (part.at[st, up, lo], ry.at[st, 0, lo]), (part.at[st, down, hi], ry.at[st, 1, hi]),
+        )[k]
+        return (src, dst, y_ss.at[st, k], y_rs.at[st, k], dev(x, down if k % 2 else up, z, c))
+
+    def y_relay(st):
+        for k, (to, rows) in enumerate(((up, lo), (down, hi))):
+            done(rh.at[st, k], y_rs.at[st, k])
+            part[st, to, rows] = (part[st, to, rows].astype(F32) + rh[st, k].astype(F32)).astype(BF16)
+            post(*y_args(st, k + 4))
+
+    def forward_group(g):
+        attn_ready(g)
+        lax.fori_loop(3 * g, 3 * g + 3, forward, 0)
+        for p in range(3):
+            aot[p, g] = dot(em[p], ao[:, g * NAT : (g + 1) * NAT], NT).astype(BF16)
+        if g == 0:
+            passed(0)
             passed(1)
+        for p in range(3):
+            grad(g, p)
 
     def d_out(i, _):
         cols = pl.ds(pl.multiple_of(i * 256, 256), 256)
         dob[:, cols] = dot(cb[...].reshape(TOK, D), wn[cols, :], NT).astype(BF16)
         return 0
 
-    lax.fori_loop(0, 3, d_out, 0)
 
     def backward(h, _):
         cols = pl.ds(pl.multiple_of(h * HDIM, HDIM), HDIM)
@@ -305,77 +315,96 @@
         gkb[:, :, cols] = (dot(ds, head(qb, h), TN) * scale).astype(BF16).reshape(FRAMES, POS, HDIM)
         return 0
 
-    y_relay(0)
-    lax.fori_loop(0, HEADS, backward, 0)
-
-    def g_args(arr, dx, kz):
+    def g_args(g, arr, dx, kz):
         px, pz = (x + dx) % 4, (zl + kz) % 2
-        src = (gqb, gkb, gvb)[arr].at[pl.ds(pl.multiple_of((px * 2 + pz) * 4, 4), 4)]
+        src = (gqb, gkb, gvb)[arr].at[pl.ds(pl.multiple_of((px * 2 + pz) * 4, 4), 4), :, pl.ds(g * NAT, NAT)]
         dst = (gq_out, gk_out, gv_out)[arr].at[
-            :, pl.ds(pl.multiple_of(x * 16, 16), 16), pl.ds(pl.multiple_of(c * HALF, HALF), HALF)
+            :, pl.ds(pl.multiple_of(x * 16, 16), 16), pl.ds(pl.multiple_of(c * HALF + g * NAT, NAT), NAT)
         ]
-        return src, dst, g_ss.at[arr, dx * 2 + kz], g_rs.at[arr, x * 2 + c], dev(px, y, zh * 2 + pz, zl)
+        i = g * 3 + arr
+        return src, dst, g_ss.at[i, dx * 2 + kz], g_rs.at[i, x * 2 + c], dev(px, y, zh * 2 + pz, zl)
 
     a_own = zl == c
 
-    def g_each(fn):
+    def g_each(g, fn):
         for arr in range(3):
             for dx in (2, 1, 3, 0):
                 for kz in (1, 0):
-                    fn(arr, dx, kz, a_own if dx == 0 and kz == 0 else None)
-
-    g_each(lambda arr, dx, kz, own: post(*g_args(arr, dx, kz), own=own))
+                    fn(g, arr, dx, kz, a_own if dx == 0 and kz == 0 else None)
+
+    def backward_group(g):
+        lax.fori_loop(3 * g, 3 * g + 3, backward, 0)
+        g_each(g, lambda g, arr, dx, kz, own: post(*g_args(g, arr, dx, kz), own=own))
+
+    def s1_rows(zz):
+        return pl.ds(pl.multiple_of(zz * 32, 32), 32)
+
+    def z_args(st, k):
+        src = s1.at[st, s1_rows((z2, z3, z1)[k]), :]
+        dst = (rzh.at[st], rz.at[st, 0], rz.at[st, 1])[k]
+        return (src, dst, z_ss.at[st, k], z_rs.at[st, k], dev(x, y, z1 if k == 2 else z3, c))
+
+    def y_sum(st):
+        for k in range(2, 6):
+            done(y_args(st, k)[1], y_rs.at[st, k])
+        total = part[st, y].astype(F32) + ry[st, 0].astype(F32) + ry[st, 1].astype(F32)
+        s1[st] = total.astype(BF16)
+        post(*z_args(st, 0))
+        post(*z_args(st, 1))
+
+    def z_relay(st):
+        done(rzh.at[st], z_rs.at[st, 0])
+        rows = s1_rows(z1)
+        s1[st, rows, :] = (s1[st, rows, :].astype(F32) + rzh[st].astype(F32)).astype(BF16)
+        post(*z_args(st, 2))
+
+    def x_args(st, kc):
+        g, p, core = st // 3, st % 3, (c + kc) % 2
+        src = s2.at[st, pl.ds(pl.multiple_of(core * 16, 16), 16), :]
+        return (src, rf.at[p, x], x_ss.at[st, kc], x_rs.at[p, x], dev(c * 2 + g, y, z, core))
+
+    def x_own(st, kc):
+        return x == c * 2 + st // 3 if kc == 0 else None
+
+    def z_sum(st):
+        for k in range(2):
+            done(rz.at[st, k], z_rs.at[st, k + 1])
+        total = s1[st, s1_rows(z), :].astype(F32)
+        s2[st] = (total + rz[st, 0].astype(F32) + rz[st, 1].astype(F32)).astype(BF16)
+        for kc in range(2):
+            post(*x_args(st, kc), own=x_own(st, kc))
+
+    forward_group(0)
+    for i in range(4):
+        done(wp.at[0, far, w_z[i]], w3_rs.at[i, 2])
+        done(wp.at[1, far, w_z[i]], w3_rs.at[i, 3])
+    lax.fori_loop(0, 6, unpack, 0)
+    y_relay(0)
     y_relay(1)
     y_relay(2)
-
-    def s1_rows(zz):
-        return pl.ds(pl.multiple_of(zz * 32, 32), 32)
-
-    def z_args(p, k):
-        src = s1.at[p, :, s1_rows((z2, z3, z1)[k]), :]
-        dst = (rzh.at[p], rz.at[p, 0], rz.at[p, 1])[k]
-        return (src, dst, z_ss.at[p, k], z_rs.at[p, k], dev(x, y, z1 if k == 2 else z3, c))
-
-    def y_sum(p):
-        total = part[p, y].astype(F32)
-        for k, dst in ((2, ry.at[p, 0, 1]), (3, ry.at[p, 1, 0]), (4, ry.at[p, 0, 0]), (5, ry.at[p, 1, 1])):
-            done(dst, y_rs.at[p, k])
-        s1[p] = (total + ry[p, 0].astype(F32) + ry[p, 1].astype(F32)).astype(BF16)
-        post(*z_args(p, 0))
-        post(*z_args(p, 1))
-
-    def z_relay(p):
-        done(rzh.at[p], z_rs.at[p, 0])
-        rows = s1_rows(z1)
-        s1[p, :, rows, :] = (s1[p, :, rows, :].astype(F32) + rzh[p].astype(F32)).astype(BF16)
-        post(*z_args(p, 2))
-
-    def x_args(p, i, kc):
-        core = (c + kc) % 2
-        src = s2.at[p, i, pl.ds(pl.multiple_of(core * 16, 16), 16), :]
-        return (src, rf.at[p, x], x_ss.at[p, i * 2 + kc], x_rs.at[p, x], dev(c * 2 + i, y, z, core))
-
-    def x_own(i, kc):
-        return x == c * 2 + i if kc == 0 else None
-
-    def z_sum(p):
-        for k in range(2):
-            done(rz.at[p, k], z_rs.at[p, k + 1])
-        total = s1[p, :, s1_rows(z), :].astype(F32)
-        s2[p] = (total + rz[p, 0].astype(F32) + rz[p, 1].astype(F32)).astype(BF16)
-        for i in range(2):
-            for kc in range(2):
-                post(*x_args(p, i, kc), own=x_own(i, kc))
-
+    lax.fori_loop(0, 3, d_out, 0)
+    backward_group(0)
+    forward_group(1)
+    y_relay(3)
     y_sum(0)
     y_sum(1)
-    z_relay(0)
     y_sum(2)
-    z_relay(1)
-    z_sum(0)
-    z_relay(2)
-    z_sum(1)
-    z_sum(2)
+    backward_group(1)
+    y_relay(4)
+    y_relay(5)
+    for st in range(3):
+        z_relay(st)
+    for st in range(3):
+        z_sum(st)
+    y_sum(3)
+    y_sum(4)
+    z_relay(3)
+    y_sum(5)
+    z_relay(4)
+    z_sum(3)
+    z_relay(5)
+    z_sum(4)
+    z_sum(5)
 
     norm = 1.0 / math.sqrt(32768.0)
     for p in range(3):
@@ -388,16 +417,14 @@
         gw_out[:, p * COL : (p + 1) * COL] = total[:12]
         gw_out[4 * p : 4 * p + 4, PK:] = total[12:]
 
-    for arr in range(3):
-        for i in range(8):
-            col = pl.ds((i % 2) * HALF, HALF)
-            done((gq_out, gk_out, gv_out)[arr].at[:, pl.ds((i // 2) * 16, 16), col], g_rs.at[arr, i])
-    g_each(lambda arr, dx, kz, own: sent(g_args(arr, dx, kz)[0], g_ss.at[arr, dx * 2 + kz], own))
-    for arr in range(5):
-        for dx in range(4):
-            for kc in range(2):
-                own = a_own if dx == 0 and kc == 0 else None
-                sent(a_args(arr, dx, kc)[0], a_ss.at[arr, dx * 2 + kc], own)
+    for g in range(2):
+        for arr in range(3):
+            for i in range(8):
+                pos = pl.ds((i // 2) * 16, 16)
+                col = pl.ds((i % 2) * HALF + g * NAT, NAT)
+                done((gq_out, gk_out, gv_out)[arr].at[:, pos, col], g_rs.at[g * 3 + arr, i])
+        g_each(g, lambda g, arr, dx, kz, own: sent(g_args(g, arr, dx, kz)[0], g_ss.at[g * 3 + arr, dx * 2 + kz], own))
+    a_sent((1, 5, 6, 7))
     for dx in range(4):
         sent(wpk, w1_ss.at[dx], w_own if dx == 0 else None)
     for i in range(3):
@@ -408,14 +435,13 @@
     for k in range(2):
         for s in range(8):
             sent(cb.at[pl.ds(s * 4, 4), :, cot_cols(c, k)], f_ss.at[k, s])
-    for p in range(3):
+    for st in range(6):
         for k in range(6):
-            sent(y_args(p, k)[0], y_ss.at[p, k])
+            sent(y_args(st, k)[0], y_ss.at[st, k])
         for k in range(3):
-            sent(z_args(p, k)[0], z_ss.at[p, k])
-        for i in range(2):
-            for kc in range(2):
-                sent(x_args(p, i, kc)[0], x_ss.at[p, i * 2 + kc], x_own(i, kc))
+            sent(z_args(st, k)[0], z_ss.at[st, k])
+        for kc in range(2):
+            sent(x_args(st, kc)[0], x_ss.at[st, kc], x_own(st, kc))
 
 
 def local(query_in, key_in, value_in, cotangent, out_weight):
@@ -441,20 +467,20 @@
             pltpu.VMEM((3, 2, ROWS, TOK), BF16),
             pltpu.VMEM((3, ROWS, NAT), BF16),
             pltpu.VMEM((4, NAT, ROWS), BF16),
-            pltpu.VMEM((3, 4, 2, 128, COL), BF16),
-            pltpu.VMEM((3, 2, 128, COL), BF16),
-            pltpu.VMEM((3, 2, 2, 128, COL), BF16),
-            pltpu.VMEM((3, 2, 128, COL), BF16),
-            pltpu.VMEM((3, 2, 32, COL), BF16),
-            pltpu.VMEM((3, 2, 2, 32, COL), BF16),
-            pltpu.VMEM((3, 2, 32, COL), BF16),
+            pltpu.VMEM((6, 4, 128, COL), BF16),
+            pltpu.VMEM((6, 2, 64, COL), BF16),
+            pltpu.VMEM((6, 2, 128, COL), BF16),
+            pltpu.VMEM((6, 128, COL), BF16),
+            pltpu.VMEM((6, 32, COL), BF16),
+            pltpu.VMEM((6, 2, 32, COL), BF16),
+            pltpu.VMEM((6, 32, COL), BF16),
             pltpu.VMEM((3, 4, 16, COL), BF16),
             pltpu.VMEM((TOK, HALF), BF16),
             pltpu.VMEM(tok, BF16), pltpu.VMEM(tok, BF16), pltpu.VMEM(tok, BF16),
-            dma((5, 8)), dma((5, 8)), dma((2, 8)), dma((2, 8)),
+            dma((8, 8)), dma((8, 8)), dma((2, 8)), dma((2, 8)),
             dma((4,)), dma((4,)), dma((3,)), dma((3,)), dma((4, 4)), dma((4, 4)),
-            dma((3, 6)), dma((3, 6)), dma((3, 3)), dma((3, 3)), dma((3, 4)), dma((3, 4)),
-            dma((3, 8)), dma((3, 8)),
+            dma((6, 6)), dma((6, 6)), dma((6, 3)), dma((6, 3)), dma((6, 2)), dma((3, 4)),
+            dma((6, 8)), dma((6, 8)),
         ],
         compiler_params=pltpu.CompilerParams(
             collective_id=0, has_side_effects=True, vmem_limit_bytes=58 * 2**20

time: 141 us -> 134 us (0.950)
  the two profiles are of different devices: /device:TPU:1 before, /device:TPU:3 now
where the time goes in v3:
time: 134 us; the launch traced here: 133 us
  Pallas kernels  128 us (96%)
  local copies, waits for them, and re-layouts  4.63 us (3%)
    pallas_call x1, Pallas kernels, local(): pl.pallas_call(kernel, out_shape=(act, act, act, jax.ShapeDtypeStruct((12...  128 us
    unnamed x10, local copies, waits for them, and re-layouts  4.63 us

profile of v3, /device:TPU:3, one launch (start us, length us, event | category | flops | bytes accessed | tf_op | source)
XLA Modules:
  0.0 133.4 jit_solution(5228751943235540283)
XLA Ops:
  0.6 128.1 %shard_map.84 = (bf16[4,64,1536]{2,1,0:T(8,128)(2,1)}, bf16[4,64,1536]{2,1,0:T(8,128)(2,1)}, bf16[4,64,1536]{2,1,0:T(8,128)(2,1)}, f32[12,3072]{1,0:T(8,128)}) custom-call(bf16[4,64,1536]{2,1,0:T(8,128)(2,1)} %bitcast.11, bf16[4,64,1536]{2,1,0:T(8,128)(2,1)} %bitcast.12, bf16[4,64,1536]{2,1,0:T(8,128)(2,1)} %bitcast.13, bf16[4,64,3072]{2,1,0:T(8,128)(2,1)} %bitcast.7, ...), custom_call_target="tpu_custom_call" | custom-call | tf_op jit(solution)/shard_map/pallas_call | solution.py:453
  128.8 0.0 copy-start.1
  128.8 0.0 copy-start
  128.8 2.2 %copy.13 = bf16[1,4,64,1536]{3,2,1,0:T(8,128)(2,1)} copy(bf16[1,4,64,1536]{3,2,1,0:T(8,128)(2,1)} %bitcast.10) | data formatting | bytes 1572864
  131.0 0.0 copy-done.1
  131.0 0.0 copy-start.2
  131.0 0.9 copy.14
  131.9 0.0 copy-done
  131.9 0.9 copy.15
  132.8 0.0 copy-done.2
  132.8 0.7 copy.16
Async XLA Ops:
  128.8 2.2 %copy-start.1 = (bf16[4,64,1536]{2,1,0:T(8,128)(2,1)S(1)}, bf16[4,64,1536]{2,1,0:T(8,128)(2,1)}, u32[]{:S(2)}) copy-start(bf16[4,64,1536]{2,1,0:T(8,128)(2,1)} %get-tuple-element.9) | copy-start | bytes 2359300
  128.8 3.1 %copy-start = (bf16[4,64,1536]{2,1,0:T(8,128)(2,1)S(1)}, bf16[4,64,1536]{2,1,0:T(8,128)(2,1)}, u32[]{:S(2)}) copy-start(bf16[4,64,1536]{2,1,0:T(8,128)(2,1)} %get-tuple-element.10) | copy-start | bytes 2359300
  131.0 1.8 %copy-start.2 = (f32[12,3072]{1,0:T(8,128)S(1)}, f32[12,3072]{1,0:T(8,128)}, u32[]{:S(2)}) copy-start(f32[12,3072]{1,0:T(8,128)} %get-tuple-element.19) | copy-start | bytes 442372

commit v4 on v3

--- a/solution.py
+++ b/solution.py
@@ -214,11 +214,11 @@
     done(wp.at[:, y, z2], w2_rs.at[2])
     w3_post(3)
     w3_relay(2)
+    w3_relay(3)
     a_sent((2, 3, 4))
     a_post((5, 6, 7), False)
     a_post((5, 6, 7), True)
     pass_on(1)
-    w3_relay(3)
 
     def attn_ready(g):
         for s in range(8):
@@ -374,16 +374,16 @@
         for kc in range(2):
             post(*x_args(st, kc), own=x_own(st, kc))
 
-    forward_group(0)
     for i in range(4):
         done(wp.at[0, far, w_z[i]], w3_rs.at[i, 2])
         done(wp.at[1, far, w_z[i]], w3_rs.at[i, 3])
     lax.fori_loop(0, 6, unpack, 0)
+    forward_group(0)
+    lax.fori_loop(0, 3, d_out, 0)
+    backward_group(0)
     y_relay(0)
     y_relay(1)
     y_relay(2)
-    lax.fori_loop(0, 3, d_out, 0)
-    backward_group(0)
     forward_group(1)
     y_relay(3)
     y_sum(0)

time: 134 us -> 132 us (0.985)
  Pallas kernels: 128 us -> 126 us
    pallas_call x1, Pallas kernels: 128 us -> 126 us  [local(): pl.pallas_call(kernel, out_shape=(act, act, act, jax.ShapeDtypeStruct((12...]
where the time goes in v4:
time: 132 us
  Pallas kernels  126 us (95%)
  local copies, waits for them, and re-layouts  4.63 us (4%)
    pallas_call x1, Pallas kernels, local(): pl.pallas_call(kernel, out_shape=(act, act, act, jax.ShapeDtypeStruct((12...  126 us
    unnamed x10, local copies, waits for them, and re-layouts  4.63 us

profile of v4, /device:TPU:3, one launch (start us, length us, event | category | flops | bytes accessed | tf_op | source)
XLA Modules:
  0.0 131.7 jit_solution(1390225826612438533)
XLA Ops:
  0.6 126.4 %shard_map.84 = (bf16[4,64,1536]{2,1,0:T(8,128)(2,1)}, bf16[4,64,1536]{2,1,0:T(8,128)(2,1)}, bf16[4,64,1536]{2,1,0:T(8,128)(2,1)}, f32[12,3072]{1,0:T(8,128)}) custom-call(bf16[4,64,1536]{2,1,0:T(8,128)(2,1)} %bitcast.11, bf16[4,64,1536]{2,1,0:T(8,128)(2,1)} %bitcast.12, bf16[4,64,1536]{2,1,0:T(8,128)(2,1)} %bitcast.13, bf16[4,64,3072]{2,1,0:T(8,128)(2,1)} %bitcast.7, ...), custom_call_target="tpu_custom_call" | custom-call | tf_op jit(solution)/shard_map/pallas_call | solution.py:453
  127.0 0.0 copy-start.1
  127.0 0.0 copy-start
  127.1 2.2 %copy.13 = bf16[1,4,64,1536]{3,2,1,0:T(8,128)(2,1)} copy(bf16[1,4,64,1536]{3,2,1,0:T(8,128)(2,1)} %bitcast.10) | data formatting | bytes 1572864
  129.2 0.0 copy-done.1
  129.2 0.0 copy-start.2
  129.2 0.9 copy.14
  130.1 0.0 copy-done
  130.1 0.9 copy.15
  131.0 0.0 copy-done.2
  131.0 0.7 copy.16
Async XLA Ops:
  127.0 2.2 %copy-start.1 = (bf16[4,64,1536]{2,1,0:T(8,128)(2,1)S(1)}, bf16[4,64,1536]{2,1,0:T(8,128)(2,1)}, u32[]{:S(2)}) copy-start(bf16[4,64,1536]{2,1,0:T(8,128)(2,1)} %get-tuple-element.9) | copy-start | bytes 2359300
  127.0 3.1 %copy-start = (bf16[4,64,1536]{2,1,0:T(8,128)(2,1)S(1)}, bf16[4,64,1536]{2,1,0:T(8,128)(2,1)}, u32[]{:S(2)}) copy-start(bf16[4,64,1536]{2,1,0:T(8,128)(2,1)} %get-tuple-element.10) | copy-start | bytes 2359300
  129.2 1.8 %copy-start.2 = (f32[12,3072]{1,0:T(8,128)S(1)}, f32[12,3072]{1,0:T(8,128)}, u32[]{:S(2)}) copy-start(f32[12,3072]{1,0:T(8,128)} %get-tuple-element.19) | copy-start | bytes 442372

commit v5 on v4

--- a/solution.py
+++ b/solution.py
@@ -295,6 +295,8 @@
         if g == 0:
             passed(0)
             passed(1)
+        else:
+            backward_group(1)
         for p in range(3):
             grad(g, p)
 
@@ -389,7 +391,6 @@
     y_sum(0)
     y_sum(1)
     y_sum(2)
-    backward_group(1)
     y_relay(4)
     y_relay(5)
     for st in range(3):

time: 132 us -> 130 us (0.985)
    pallas_call x1, Pallas kernels: 126 us -> 125 us  [local(): pl.pallas_call(kernel, out_shape=(act, act, act, jax.ShapeDtypeStruct((12...]
where the time goes in v5:
time: 130 us
  Pallas kernels  125 us (96%)
  local copies, waits for them, and re-layouts  4.63 us (4%)
    pallas_call x1, Pallas kernels, local(): pl.pallas_call(kernel, out_shape=(act, act, act, jax.ShapeDtypeStruct((12...  125 us
    unnamed x10, local copies, waits for them, and re-layouts  4.63 us

profile of v5, /device:TPU:3, one launch (start us, length us, event | category | flops | bytes accessed | tf_op | source)
XLA Modules:
  0.0 129.9 jit_solution(16915031685451401618)
XLA Ops:
  0.6 124.6 %shard_map.84 = (bf16[4,64,1536]{2,1,0:T(8,128)(2,1)}, bf16[4,64,1536]{2,1,0:T(8,128)(2,1)}, bf16[4,64,1536]{2,1,0:T(8,128)(2,1)}, f32[12,3072]{1,0:T(8,128)}) custom-call(bf16[4,64,1536]{2,1,0:T(8,128)(2,1)} %bitcast.11, bf16[4,64,1536]{2,1,0:T(8,128)(2,1)} %bitcast.12, bf16[4,64,1536]{2,1,0:T(8,128)(2,1)} %bitcast.13, bf16[4,64,3072]{2,1,0:T(8,128)(2,1)} %bitcast.7, ...), custom_call_target="tpu_custom_call" | custom-call | tf_op jit(solution)/shard_map/pallas_call | solution.py:454
  125.3 0.0 copy-start.1
  125.3 0.0 copy-start
  125.3 2.2 %copy.13 = bf16[1,4,64,1536]{3,2,1,0:T(8,128)(2,1)} copy(bf16[1,4,64,1536]{3,2,1,0:T(8,128)(2,1)} %bitcast.10) | data formatting | bytes 1572864
  127.5 0.0 copy-done.1
  127.5 0.0 copy-start.2
  127.5 0.9 copy.14
  128.3 0.0 copy-done
  128.3 0.9 copy.15
  129.2 0.0 copy-done.2
  129.2 0.7 copy.16
Async XLA Ops:
  125.3 2.2 %copy-start.1 = (bf16[4,64,1536]{2,1,0:T(8,128)(2,1)S(1)}, bf16[4,64,1536]{2,1,0:T(8,128)(2,1)}, u32[]{:S(2)}) copy-start(bf16[4,64,1536]{2,1,0:T(8,128)(2,1)} %get-tuple-element.9) | copy-start | bytes 2359300
  125.3 3.1 %copy-start = (bf16[4,64,1536]{2,1,0:T(8,128)(2,1)S(1)}, bf16[4,64,1536]{2,1,0:T(8,128)(2,1)}, u32[]{:S(2)}) copy-start(bf16[4,64,1536]{2,1,0:T(8,128)(2,1)} %get-tuple-element.10) | copy-start | bytes 2359300
  127.5 1.8 %copy-start.2 = (f32[12,3072]{1,0:T(8,128)S(1)}, f32[12,3072]{1,0:T(8,128)}, u32[]{:S(2)}) copy-start(f32[12,3072]{1,0:T(8,128)} %get-tuple-element.19) | copy-start | bytes 442372
